TPU v7x, 256 devices: a whole 4x4x8 slice. The times are simulated.
256 devices in a mesh: cam: 8 (over z), frame: 16 (over x, y_hi, core), head: 2 (over y_lo).
Axes of the slice: x: 4, y: 4 (y_hi: 2, y_lo: 2; y = y_hi * 2 + y_lo), z: 8, core: 2. Of those that a mesh axis runs over, the one named last changes fastest.
Arguments:
- queries: bfloat16 [8, 32, 4, 64, 1024], P('cam', 'frame', None, None, 'head'), may hold values from -8 to 8
- keys: bfloat16 [8, 32, 4, 64, 1024], P('cam', 'frame', None, None, 'head'), may hold values from -8 to 8
- values: bfloat16 [8, 32, 4, 64, 1024], P('cam', 'frame', None, None, 'head'), may hold values from -3 to 3
- offsets: int32 [8, 2], replicated, may hold values from 0 to 16
- w_out: bfloat16 [1024, 2048], P('head'), may hold values from -0.1875 to 0.1875
- grad_out: bfloat16 [8, 32, 2, 4, 16, 2048], P('cam', 'frame', None, None, None, 'head'), may hold values from -6 to 6
Outputs:
- layer_out: bfloat16 [8, 32, 2, 4, 16, 2048], P('cam', 'frame', None, None, None, 'head')
- grad_queries: float32 [8, 32, 4, 64, 1024], P('cam', 'frame', None, None, 'head')
- grad_keys: float32 [8, 32, 4, 64, 1024], P('cam', 'frame', None, None, 'head')
- grad_values: float32 [8, 32, 4, 64, 1024], P('cam', 'frame', None, None, 'head')
- grad_w_out: float32 [1024, 2048], P('head')
Inputs may be any that keep to these rules, and one draw needn't show every extreme that they name: offsets[c,0] places camera c's strip toward camera c+1 at 32 + offsets[c,0]; offsets[c,1] places camera c+1's strip toward camera c at offsets[c,1].
All inputs are finite; a program needn't handle non-finite values.
Results may differ from a plain program's by a relative error of at most 0.04.
Values may be sent and summed in bfloat16 or wider, within the bound.
A program may use at most 128 MiB of HBM per device.

v0:
```python
import jax
import jax.numpy as jnp
from jax import lax
from jax.sharding import PartitionSpec as P

HD = 128


def from_behind(array, axis, by):
    devices = lax.axis_size(axis)
    return lax.ppermute(array, axis, [(i, (i + by) % devices) for i in range(devices)])


def strip_rows(grid_field, first_col, strip_width):
    cut_block = lax.dynamic_slice_in_dim(grid_field, first_col, strip_width, 3)
    return cut_block.reshape(-1, grid_field.shape[-1])


def on_device(queries, keys, values, offsets, w_out, grad_out):
    cam_count = lax.axis_size("cam")
    cam_index = lax.axis_index("cam")
    field_shape = queries.shape
    grid_width = field_shape[3]
    strip_width = grid_width // 4
    heads_local = field_shape[4] // HD
    frames_local = field_shape[1]
    score_scale = HD ** (-0.5)
    right_first = grid_width // 2 + offsets[cam_index, 0]
    left_first = offsets[(cam_index + cam_count - 1) % cam_count, 1]

    def sides_of(grid_field):
        return jnp.stack(
            [
                strip_rows(grid_field, left_first, strip_width),
                strip_rows(grid_field, right_first, strip_width),
            ]
        )

    def split_heads(matrix):
        return matrix.reshape(matrix.shape[0], matrix.shape[1], heads_local, HD)

    query_sides = sides_of(queries)
    key_sides = sides_of(keys)
    value_sides = sides_of(values)
    row_count = query_sides.shape[1]
    prev_keys, prev_values = from_behind((key_sides[1], value_sides[1]), "cam", 1)
    next_keys, next_values = from_behind((key_sides[0], value_sides[0]), "cam", -1)
    near_keys = jnp.stack([prev_keys, next_keys])
    near_values = jnp.stack([prev_values, next_values])
    far_keys, far_values = (
        lax.all_gather(near_keys, "frame", axis=1, tiled=True),
        lax.all_gather(near_values, "frame", axis=1, tiled=True),
    )
    full_grad = lax.all_gather(grad_out, "head", axis=5, tiled=True)
    grad_rows = full_grad.reshape(-1, full_grad.shape[-1])
    grad_attn = jnp.einsum(
        "td,ed->te", grad_rows, w_out, preferred_element_type=jnp.float32
    ).astype(jnp.bfloat16)
    query_heads = split_heads(query_sides)
    shaped = grad_attn.reshape(frames_local, 2, -1, grad_attn.shape[-1])
    grad_heads = split_heads(
        jnp.transpose(shaped, (1, 0, 2, 3)).reshape(2, -1, grad_attn.shape[-1])
    )
    key_heads = split_heads(far_keys)
    value_heads = split_heads(far_values)
    scores = (
        jnp.einsum("sqhd,skhd->shqk", query_heads, key_heads, preferred_element_type=jnp.float32)
        * score_scale
    )
    row_max = jnp.max(scores, axis=-1, keepdims=True)
    exp_scores = jnp.exp(scores - row_max)
    row_total = jnp.sum(exp_scores, axis=-1, keepdims=True)
    prob_full = exp_scores / row_total
    weights = prob_full.astype(jnp.bfloat16)
    attended = jnp.einsum(
        "shqk,skhd->sqhd", weights, value_heads, preferred_element_type=jnp.float32
    ).astype(jnp.bfloat16)
    matrix = attended.reshape(2, row_count, -1)
    shaped = matrix.reshape(2, frames_local, -1, matrix.shape[-1])
    attn_rows = jnp.transpose(shaped, (1, 0, 2, 3)).reshape(-1, matrix.shape[-1])
    partial_out = jnp.dot(attn_rows, w_out, preferred_element_type=jnp.float32)
    out_rows = lax.psum_scatter(partial_out, "head", scatter_dimension=1, tiled=True).astype(
        jnp.bfloat16
    )
    layer_out = out_rows.reshape(grad_out.shape)
    local_weight = jnp.einsum("te,td->ed", attn_rows, grad_rows, preferred_element_type=jnp.float32)
    grad_w_out = lax.psum(local_weight, ("cam", "frame"))
    row_delta = jnp.sum(grad_heads.astype(jnp.float32) * attended.astype(jnp.float32), axis=-1)
    row_delta = jnp.transpose(row_delta, (0, 2, 1))[..., None]
    grad_prob = jnp.einsum(
        "sqhd,skhd->shqk", grad_heads, value_heads, preferred_element_type=jnp.float32
    )
    grad_score = (prob_full * (grad_prob - row_delta) * score_scale).astype(jnp.bfloat16)
    grad_query = jnp.einsum(
        "shqk,skhd->sqhd", grad_score, key_heads, preferred_element_type=jnp.float32
    )
    grad_query = grad_query.reshape(2, row_count, -1)
    key_term = jnp.einsum(
        "shqk,sqhd->kshd", grad_score, query_heads, preferred_element_type=jnp.float32
    )
    value_term = jnp.einsum(
        "shqk,sqhd->kshd", weights, grad_heads, preferred_element_type=jnp.float32
    )
    summed = lax.psum_scatter(
        jnp.stack([key_term, value_term], axis=1).reshape(row_count * lax.axis_size("frame"), -1),
        "frame",
        scatter_dimension=0,
        tiled=True,
    )
    pair_grads = summed.reshape(row_count, 2, 2, -1)
    right_grads = from_behind(pair_grads[:, :, 0], "cam", -1)
    left_grads = from_behind(pair_grads[:, :, 1], "cam", 1)
    own_key_grad = jnp.stack([left_grads[:, 0], right_grads[:, 0]])
    own_value_grad = jnp.stack([left_grads[:, 1], right_grads[:, 1]])

    def place_sides(side_rows):
        full_grid = jnp.zeros(field_shape, jnp.float32)
        blocks = side_rows.reshape(
            2, field_shape[0], field_shape[1], field_shape[2], strip_width, field_shape[4]
        )
        full_grid = lax.dynamic_update_slice_in_dim(full_grid, blocks[0], left_first, 3)
        return lax.dynamic_update_slice_in_dim(full_grid, blocks[1], right_first, 3)

    return (
        layer_out,
        place_sides(grad_query),
        place_sides(own_key_grad),
        place_sides(own_value_grad),
        grad_w_out,
    )


def solution(mesh):
    return jax.shard_map(
        on_device,
        mesh=mesh,
        in_specs=(
            P("cam", "frame", None, None, "head"),
            P("cam", "frame", None, None, "head"),
            P("cam", "frame", None, None, "head"),
            P(),
            P("head", None),
            P("cam", "frame", None, None, None, "head"),
        ),
        out_specs=(
            P("cam", "frame", None, None, None, "head"),
            P("cam", "frame", None, None, "head"),
            P("cam", "frame", None, None, "head"),
            P("cam", "frame", None, None, "head"),
            P("head", None),
        ),
        check_vma=False,
    )
```

profile of v0, /device:TPU:1, one launch (start us, length us, event | category | flops | bytes accessed | tf_op | source)
XLA Modules:
  0.0 1676.0 jit_solution(11193615144946810085)
XLA Ops:
  13.9 6.5 collective-permute-start.3
  20.5 2.2 collective-permute-done.3
  22.6 2.9 collective-permute-done.2
  29.0 2.8 collective-permute-done.1
  34.2 5.8 all-gather.8.cloned.1.call-done
  42.3 63.6 %all-gather.6.cloned.1.call-done = bf16[2,2048,512]{2,1,0:T(8,128)(2,1)} async-done(((bf16[2,128,512]{2,1,0:T(8,128)(2,1)}), bf16[2,2048,512]{2,1,0:T(8,128)(2,1)}) %all-gather.6.cloned.1.call-update) | async-done | bytes 4194320 | tf_op jit(solution)/shard_map/all_gather | solution.py:51
  106.0 6.3 copy.43
  112.2 8.3 fusion.14
  120.5 4.7 fusion.5
  125.2 2.1 copy-done.1
  127.3 4.6 convolution_bitcast_fusion
  131.9 37.4 %all-gather.4.cloned.1.call-done = bf16[2,2048,512]{2,1,0:T(8,128)(2,1)} async-done(((bf16[2,128,512]{2,1,0:T(8,128)(2,1)}), bf16[2,2048,512]{2,1,0:T(8,128)(2,1)}) %all-gather.4.cloned.1.call-update) | async-done | bytes 4194320 | tf_op jit(solution)/shard_map/all_gather | solution.py:52
  169.3 6.2 copy.40
  175.5 4.9 multiply_reduce_fusion.1
  180.4 4.6 multiply_convert_fusion
  187.1 6.2 pad_maximum_fusion
  193.7 2.0 fusion.15
  196.0 2.7 fusion.16
  198.8 147.5 %reduce-scatter.5.cloned.1.call-done = f32[128,2048]{0,1:T(8,128)} async-done(((f32[2048,2048]{0,1:T(8,128)}), f32[128,2048]{0,1:T(8,128)}) %reduce-scatter.5.cloned.1.call-update) | async-done | bytes 1048592 | tf_op jit(solution)/shard_map/reduce_scatter | solution.py:104
  352.6 4.7 convolution_bitcast_fusion.2
  362.4 21.8 %reduce-scatter.3.cloned.1.call-done = f32[256,1024]{1,0:T(8,128)} async-done(((f32[256,2048]{1,0:T(8,128)}), f32[256,1024]{1,0:T(8,128)}) %reduce-scatter.3.cloned.1.call-update) | async-done | bytes 1048592 | tf_op jit(solution)/shard_map/reduce_scatter | solution.py:82
  384.2 2.1 convert_element_type.27
  395.0 1269.5 %all-reduce.2.cloned.1.call-done = f32[512,2048]{1,0:T(8,128)} async-done(((f32[512,2048]{1,0:T(8,128)}), f32[512,2048]{1,0:T(8,128)}) %all-reduce.2.cloned.1.call-update) | async-done | bytes 4194320 | tf_op jit(solution)/shard_map/psum | solution.py:87
  1664.4 4.7 copy.76
  (74 shorter events, 34.3 us)
Async XLA Ops:
  7.2 32.9 %copy-start = (bf16[512,2048]{1,0:T(8,128)(2,1)S(1)}, bf16[512,2048]{1,0:T(8,128)(2,1)}, u32[]{:S(2)}) copy-start(bf16[512,2048]{1,0:T(8,128)(2,1)} %param.10) | copy-start | bytes 6291460
  7.2 32.9 %all-gather.8.cloned.1.call-start = ((), (), s32[]{:S(2)}) async-start(), calls=%async_computation.5 | async-start | bytes 1572864 | tf_op jit(solution)/shard_map/all_gather | solution.py:54
  7.9 98.0 %all-gather.6.cloned.1.call-start = ((), (), s32[]{:S(2)}) async-start(), calls=%async_computation.3 | async-start | bytes 4456448 | tf_op jit(solution)/shard_map/all_gather | solution.py:51
  13.9 8.7 collective-permute-start.3
  20.5 5.0 collective-permute-start.2
  26.2 143.1 %all-gather.4.cloned.1.call-start = ((), (), s32[]{:S(2)}) async-start(), calls=%async_computation.2 | async-start | bytes 4456448 | tf_op jit(solution)/shard_map/all_gather | solution.py:52
  27.4 4.3 collective-permute-start.1
  28.1 5.0 collective-permute-start
  33.8 312.4 %reduce-scatter.5.cloned.1.call-start = ((), (), s32[]{:S(2)}) async-start(), calls=%async_computation.6 | async-start | bytes 17825792 | tf_op jit(solution)/shard_map/reduce_scatter | solution.py:104
  125.2 2.1 copy-start.1
  175.5 4.9 copy-start.3
  175.5 11.6 slice-start
  180.4 6.7 slice-start.1
  185.1 2.0 copy-start.2
  193.3 190.9 %reduce-scatter.3.cloned.1.call-start = ((), (), s32[]{:S(2)}) async-start(), calls=%async_computation.4 | async-start | bytes 3145728 | tf_op jit(solution)/shard_map/reduce_scatter | solution.py:82
  193.7 2.3 copy-start.6
  195.7 1468.7 %all-reduce.2.cloned.1.call-start = ((), (), s32[]{:S(2)}) async-start(), calls=%async_computation.7 | async-start | bytes 8388608 | tf_op jit(solution)/shard_map/psum | solution.py:87
  348.5 37.7 %collective-permute-start.4 = (f32[128,2,512]{2,0,1:T(8,128)}, f32[128,2,512]{2,0,1:T(8,128)}, u32[]{:S(2)}, u32[]{:S(2)}) collective-permute-start(f32[128,2,512]{2,0,1:T(8,128)} %bitcast.91), channel_id=1, source_target_pairs={{0,32},{32,64},{64,96},{96,128},{128,160},{160,192},{192,224},{224... | collective-permute-start | bytes 1572872 | tf_op jit(solution)/shard_map/ppermute | solution.py:11
  350.8 38.6 %collective-permute-start.5 = (f32[128,2,512]{2,0,1:T(8,128)}, f32[128,2,512]{2,0,1:T(8,128)}, u32[]{:S(2)}, u32[]{:S(2)}) collective-permute-start(f32[128,2,512]{2,0,1:T(8,128)} %bitcast.32), channel_id=1, source_target_pairs={{0,224},{32,0},{64,32},{96,64},{128,96},{160,128},{192,160},{224,1... | collective-permute-start | bytes 1572872 | tf_op jit(solution)/shard_map/ppermute | solution.py:11
  392.4 1.0 copy-start.5
  395.0 1274.2 %copy-start.4 = (f32[1,2,4,64,512]{4,3,2,1,0:T(8,128)}, f32[1,2,4,64,512]{4,3,2,1,0:T(8,128)S(1)}, u32[]{:S(2)}) copy-start(f32[1,2,4,64,512]{4,3,2,1,0:T(8,128)S(1)} %dynamic_update_slice.23) | copy-start | bytes 3145732
Sparse Core Ops, SparseCore 0:
  9.8 30.1 all-gather.7
  43.4 62.5 all-gather.5
  109.3 59.9 all-gather.3
  193.4 152.8 reduce-scatter.4
  348.8 35.3 reduce-scatter.2
  386.7 1277.7 all-reduce.1
where the time goes:
time: 1680 us
  waiting for transfers between devices  1560 us (93%)
  local copies, waits for them, and re-layouts  41.5 us (2%)
  matrix products  35.1 us (2%)
  between operations  17.7 us (1%)
    psum x1, waiting for transfers between devices, on_device(): grad_w_out = lax.psum(local_weight, ('cam', 'frame'))  1270 us
    reduce_scatter x1, waiting for transfers between devices, on_device(): lax.psum_scatter(jnp.stack([key_term, value_term], axis=1).reshape(row_co...  147 us
    all_gather x1, waiting for transfers between devices, on_device(): lax.all_gather(near_keys, 'frame', axis=1, tiled=True)  63.6 us
    all_gather x1, waiting for transfers between devices, on_device(): lax.all_gather(near_values, 'frame', axis=1, tiled=True)  37.4 us
  transfers between devices with their start and end apart: 12, of which 10 were waited for; matrix products, arithmetic and copies ran while one was open for 4% of the time, Pallas kernels for 0%

commit v1 on v0

v1 whole, which is shorter than its diff:
```python
import functools

import jax
import jax.numpy as jnp
from jax import lax
from jax.experimental import pallas as pl
from jax.experimental.pallas import tpu as pltpu
from jax.sharding import PartitionSpec as P

HD = 128
BF = jnp.bfloat16
F32 = jnp.float32
MESH = pl.DeviceIdType.MESH
LOG2E = 1.4426950408889634
NT = (((1,), (1,)), ((), ()))


def dot(a, b):
    return jnp.dot(a, b, preferred_element_type=F32)


def dot_nt(a, b):
    return lax.dot_general(a, b, NT, preferred_element_type=F32)


def each(count, fn):
    def step(i, carry):
        fn(i)
        return carry

    lax.fori_loop(0, count, step, 0)


def transposed(block):
    return block.astype(F32).T


def selector(off):
    rows = lax.broadcasted_iota(jnp.int32, (128, 256), 0)
    cols = lax.broadcasted_iota(jnp.int32, (128, 256), 1)
    hit = cols == rows + (lax.shift_right_logical(rows, 4) * 16 + off)
    return jnp.where(hit, 1.0, 0.0).astype(BF)


def selector_t(off):
    rows = lax.broadcasted_iota(jnp.int32, (256, 128), 1)
    cols = lax.broadcasted_iota(jnp.int32, (256, 128), 0)
    hit = cols == rows + (lax.shift_right_logical(rows, 4) * 16 + off)
    return jnp.where(hit, 1.0, 0.0).astype(BF)


def main_kernel(
    offs, q_hbm, k_hbm, v_hbm, w_hbm, g_hbm,
    lo_out, dq_out, dkv_out, gw_out,
    q_in, k_in, v_in, w, gfull,
    q_send, kv_send, do_send, q_recv, kv_recv, do_recv,
    kt, vt, probs, o_t, rl,
    att_send, att_recv, dq_send, dk_acc, dv_acc, dkv_send,
    a_rows, a_t, core_send, core_recv, own, lo_send, lo_recv,
    x_send, x_recv, vx, z_send, z_recv, y_send, y_recv,
    in_sem, g_ss, g_rs, q_ss, q_rs, kv_ss, kv_rs, do_ss, do_rs,
    att_ss, att_rs, dq_ss, dq_rs, dkv_ss, dkv_rs, core_ss, core_rs, lo_ss, lo_rs,
    x_ss, x_rs, z_ss, z_rs, y_ss, y_rs, zg_ss, zg_rs, xg_ss, xg_rs, xf_ss, xf_rs,
    cg_ss, cg_rs,
):
    c = lax.axis_index("cam")
    f = lax.axis_index("frame")
    hh = lax.axis_index("head")
    x, yh, k = f // 4, (f // 2) % 2, f % 2
    u = x * 2 + k
    scale = HD ** (-0.5)

    def frame_of(unit):
        return (unit // 2) * 4 + yh * 2 + unit % 2

    def frame_x(to_x):
        return to_x * 4 + yh * 2 + k

    def remote(src, dst, ss, rs, **where):
        return pltpu.make_async_remote_copy(
            src_ref=src, dst_ref=dst, send_sem=ss, recv_sem=rs,
            device_id=where, device_id_type=MESH)

    other_core = x * 4 + yh * 2 + 1 - k
    other_half = x * 4 + (1 - yh) * 2 + k
    xp, xm, xo = (x + 1) % 4, (x + 3) % 4, (x + 2) % 4

    barrier = pltpu.get_barrier_semaphore()

    def greet(**where):
        pl.semaphore_signal(barrier, inc=1, device_id=where, device_id_type=MESH)

    def greet_cams(i):
        greet(cam=(c + 1) % 8, frame=i)
        greet(cam=(c + 7) % 8, frame=i)

    loads = [
        pltpu.make_async_copy(src, dst, in_sem.at[i])
        for i, (src, dst) in enumerate(
            ((k_hbm, k_in), (v_hbm, v_in), (q_hbm, q_in), (g_hbm, gfull.at[hh]), (w_hbm, w)))
    ]
    for load in loads:
        load.start()
    each(16, greet_cams)
    each(7, lambda i: greet(frame=frame_of((u + 1 + i) % 8)))
    each(5, lambda i: greet(cam=(c + 2 + i) % 8))
    greet(frame=other_half)
    greet(head=1 - hh)

    off = (offs[(c + 7) % 8, 1], offs[c, 0])
    sel = [selector(o) for o in off]

    def strip(ref, side):
        window = ref[:, :, side * 32:(side + 1) * 32, :].reshape(256, 512)
        return dot(sel[side], window).astype(BF)

    for i, ref in enumerate((k_in, v_in)):
        loads[i].wait()
        for side in range(2):
            cut = strip(ref, side)
            for h in range(4):
                kv_send[(1 - side) * 4 + h, i] = cut[:, h * 128:(h + 1) * 128]

    pl.semaphore_wait(barrier, 46)

    def kv_copy(i):
        unit, half = (u + i // 2) % 8, (yh + i) % 2
        to_cam = (c + 9 - 2 * (unit // 4)) % 8
        to_frame = (unit // 2) * 4 + half * 2 + unit % 2
        return remote(kv_send.at[unit], kv_recv.at[f], kv_ss.at[i], kv_rs.at[f],
                      cam=to_cam, frame=to_frame)

    each(16, lambda i: kv_copy(i).start())

    loads[2].wait()
    for side in range(2):
        cut = strip(q_in, side)
        for h in range(4):
            q_send[side * 4 + h] = cut[:, h * 128:(h + 1) * 128]

    def half_copy(send, recv, ss, rs, i):
        unit = (u + i) % 8
        return remote(send.at[unit], recv.at[u], ss.at[unit], rs.at[u], frame=frame_of(unit))

    def own_copy(send, recv, rs):
        return pltpu.make_async_copy(send.at[u], recv.at[u], rs.at[u])

    own_copy(q_send, q_recv, q_rs).start()
    each(7, lambda i: half_copy(q_send, q_recv, q_ss, q_rs, i + 1).start())
    loads[3].wait()
    g_copy = remote(gfull.at[hh], gfull.at[hh], g_ss, g_rs, head=1 - hh)
    g_copy.start()

    def arrived(ref, sem):
        pltpu.make_async_copy(ref, ref, sem).wait()

    def kv_arrive(i):
        arrived(kv_recv.at[i], kv_rs.at[i])
        cols = pl.ds(pl.multiple_of(i * 128, 128), 128)
        kt[:, cols] = transposed(kv_recv[i, 0]).astype(BF)
        vt[:, cols] = transposed(kv_recv[i, 1]).astype(BF)

    each(16, kv_arrive)

    def send_block(send, recv, ss, rs, unit):
        @pl.when(unit == u)
        def _():
            own_copy(send, recv, rs).start()

        @pl.when(unit != u)
        def _():
            remote(send.at[unit], recv.at[u], ss.at[unit], rs.at[u],
                   frame=frame_of(unit)).start()

    def forward(i):
        b = (x + i) % 4
        for t in range(2):
            arrived(q_recv.at[2 * b + t], q_rs.at[2 * b + t])
        queries = q_recv[pl.ds(2 * b, 2)].reshape(256, 128)
        scores = dot_nt(kv_recv[:, 0].reshape(2048, 128), queries)
        top = jnp.max(scores, axis=0, keepdims=True)
        weights = jnp.exp2((scores - top) * (scale * LOG2E))
        inverse = 1.0 / jnp.sum(weights, axis=0, keepdims=True)
        weights = weights.astype(BF)
        probs[b] = weights
        out_t = dot(vt[...], weights) * inverse
        o_t[b] = out_t
        rl[b] = inverse
        att_send[pl.ds(2 * b, 2)] = out_t.T.astype(BF).reshape(2, 128, 128)
        for t in range(2):
            send_block(att_send, att_recv, att_ss, att_rs, 2 * b + t)

    each(4, forward)

    arrived(gfull.at[1 - hh], g_rs)
    loads[4].wait()
    grad_attn = dot_nt(gfull[0], w[:, :1024]) + dot_nt(gfull[1], w[:, 1024:])
    grad_attn = grad_attn.astype(BF)
    for fr in range(2):
        for s in range(2):
            for h in range(4):
                do_send[s * 4 + h, fr * 64:(fr + 1) * 64] = grad_attn[
                    fr * 128 + s * 64:fr * 128 + s * 64 + 64, h * 128:(h + 1) * 128]
    own_copy(do_send, do_recv, do_rs).start()
    each(7, lambda i: half_copy(do_send, do_recv, do_ss, do_rs, i + 1).start())

    each(8, lambda i: arrived(att_recv.at[i], att_rs.at[i]))
    for fr in range(2):
        for s in range(2):
            for h in range(4):
                a_rows[fr * 128 + s * 64:fr * 128 + s * 64 + 64, h * 128:(h + 1) * 128] = att_recv[
                    s * 4 + h, fr * 64:(fr + 1) * 64]
    for fr in range(2):
        for h in range(4):
            a_t[h * 128:(h + 1) * 128, fr * 128:(fr + 1) * 128] = transposed(
                a_rows[fr * 128:(fr + 1) * 128, h * 128:(h + 1) * 128]).astype(BF)

    theirs = a_t[pl.ds(pl.multiple_of((1 - k) * 256, 256), 256), :]
    for j in range(2):
        core_send[j] = dot(theirs, gfull[j]).astype(BF)
        remote(core_send.at[j], core_recv.at[j], core_ss.at[j], core_rs.at[j],
               frame=other_core).start()

    lo_send[...] = dot(
        a_rows[...], w[:, pl.ds(pl.multiple_of((1 - hh) * 1024, 1024), 1024)]).astype(BF)
    lo_copy = remote(lo_send, lo_recv, lo_ss, lo_rs, head=1 - hh)
    lo_copy.start()

    mine = a_t[pl.ds(pl.multiple_of(k * 256, 256), 256), :]
    for j in range(2):
        own[:, j * 1024:(j + 1) * 1024] = dot(mine, gfull[j])
    for j in range(2):
        arrived(core_recv.at[j], core_rs.at[j])
        own[:, j * 1024:(j + 1) * 1024] += core_recv[j].astype(F32)

    def rows_of(chunk, half):
        return own[pl.ds(pl.multiple_of(chunk * 64 + half * 32, 32), 32), :]

    def x_copy(slot, to_x):
        return remote(x_send.at[slot], x_recv.at[slot], x_ss.at[slot], x_rs.at[slot],
                      frame=frame_x(to_x))

    for slot, (chunk, half, to_x) in enumerate(((xo, 0, xp), (xo, 1, xm), (xp, 1, xp), (xm, 0, xm))):
        x_send[slot] = rows_of(chunk, half).astype(BF)
        x_copy(slot, to_x).start()

    def backward(i):
        b = (x + i) % 4
        for t in range(2):
            arrived(do_recv.at[2 * b + t], do_rs.at[2 * b + t])
        queries = q_recv[pl.ds(2 * b, 2)].reshape(256, 128)
        weights = probs[b]
        grad_t = transposed(do_recv[pl.ds(2 * b, 2)].reshape(256, 128)) * rl[b]
        delta = jnp.sum(grad_t * o_t[b], axis=0, keepdims=True)
        grads = grad_t.T.astype(BF)
        grad_probs = dot(kv_recv[:, 1].reshape(2048, 128), grad_t.astype(BF))
        grad_scores = (weights.astype(F32) * (grad_probs - delta)).astype(BF)
        grad_q_t = dot(kt[...], grad_scores) * scale
        dq_send[pl.ds(2 * b, 2)] = grad_q_t.T.astype(BF).reshape(2, 128, 128)
        for t in range(2):
            send_block(dq_send, dq_out, dq_ss, dq_rs, 2 * b + t)
        dk_acc[...] += dot(grad_scores, queries)
        dv_acc[...] += dot(weights, grads)

    dk_acc[...] = jnp.zeros_like(dk_acc)
    dv_acc[...] = jnp.zeros_like(dv_acc)
    each(2, backward)

    for slot, (chunk, half, to_x) in enumerate(((xp, 0, xp), (xm, 1, xm))):
        arrived(x_recv.at[slot], x_rs.at[slot])
        x_send[4 + slot] = (rows_of(chunk, half) + x_recv[slot].astype(F32)).astype(BF)
        x_copy(4 + slot, to_x).start()

    each(2, lambda i: backward(i + 2))
    dkv_send[:, 0] = (dk_acc[...] * scale).astype(BF).reshape(16, 128, 128)
    dkv_send[:, 1] = dv_acc[...].astype(BF).reshape(16, 128, 128)

    def dkv_copy(i):
        to_frame = (f + i) % 16
        to_cam = (c + 7 + 2 * (x // 2)) % 8
        return remote(dkv_send.at[to_frame], dkv_out.at[yh, u], dkv_ss.at[i],
                      dkv_rs.at[yh * 8 + u], cam=to_cam, frame=to_frame)

    for slot in range(2, 6):
        arrived(x_recv.at[slot], x_rs.at[slot])
    vx[0:32] = rows_of(x, 0) + x_recv[3].astype(F32) + x_recv[4].astype(F32)
    vx[32:64] = rows_of(x, 1) + x_recv[2].astype(F32) + x_recv[5].astype(F32)
    for i in range(8):
        z_send[i] = vx[:, i * 256:(i + 1) * 256].astype(BF)

    def z_copy(i):
        to = (c + i) % 8
        return remote(z_send.at[to], z_recv.at[c], z_ss.at[to], z_rs.at[c], cam=to)

    each(7, lambda i: z_copy(i + 1).start())
    each(16, lambda i: dkv_copy(i).start())

    here = dot(a_rows[...], w[:, pl.ds(pl.multiple_of(hh * 1024, 1024), 1024)])
    lo_copy.wait()
    lo_out[...] = (here + lo_recv[...].astype(F32)).astype(BF)

    total = vx[:, pl.ds(pl.multiple_of(c * 256, 256), 256)]
    for i in range(1, 8):
        frm = (c + i) % 8
        arrived(z_recv.at[frm], z_rs.at[frm])
        total = total + z_recv[frm].astype(F32)
    y_send[...] = total.astype(BF)
    y_copy = remote(y_send, y_recv, y_ss, y_rs, frame=other_half)
    y_copy.start()
    y_copy.wait()
    gw_out[k, x, c] = (y_send[...].astype(F32) + y_recv[...].astype(F32)).astype(BF)

    def zg_copy(i):
        return remote(gw_out.at[k, x, c], gw_out.at[k, x, c], zg_ss.at[i], zg_rs.at[c],
                      cam=(c + i) % 8)

    def xg_copy(z, side):
        return remote(gw_out.at[k, x, z], gw_out.at[k, x, z], xg_ss.at[side, z], xg_rs.at[side, z],
                      frame=frame_x(xp if side == 0 else xm))

    def xf_copy(z):
        odd = z % 2
        src = gw_out.at[k, (x + 3 + 2 * odd) % 4, z]
        return remote(src, src, xf_ss.at[z], xf_rs.at[z], frame=frame_x((x + 1 + 2 * odd) % 4))

    def cg_copy(to_x, slot):
        part = gw_out.at[k, to_x]
        return remote(part, part, cg_ss.at[slot], cg_rs.at[slot], frame=other_core)

    each(7, lambda i: zg_copy(i + 1).start())
    order = (0, 1, 7, 2, 6, 3, 5, 4)
    for d in order:
        z = (c + d) % 8
        if d:
            arrived(gw_out.at[k, x, z], zg_rs.at[z])
        xg_copy(z, 0).start()
        xg_copy(z, 1).start()
    cg_copy(x, 0).start()
    for d in order:
        z = (c + d) % 8
        arrived(gw_out.at[k, xm, z], xg_rs.at[0, z])
        arrived(gw_out.at[k, xp, z], xg_rs.at[1, z])
        xf_copy(z).start()
    cg_copy(xm, 1).start()
    cg_copy(xp, 2).start()
    each(8, lambda z: arrived(gw_out.at[k, xo, z], xf_rs.at[z]))
    cg_copy(xo, 3).start()

    each(8, lambda i: arrived(dq_out.at[i], dq_rs.at[i]))
    each(16, lambda i: arrived(dkv_out.at[i // 8, i % 8], dkv_rs.at[i]))
    for slot, at in enumerate((x, xm, xp, xo)):
        arrived(gw_out.at[1 - k, at], cg_rs.at[slot])

    g_copy.wait_send()
    each(16, lambda i: kv_copy(i).wait_send())

    def sent(send, recv, ss, rs):
        each(7, lambda i: half_copy(send, recv, ss, rs, i + 1).wait_send())

    sent(q_send, q_recv, q_ss, q_rs)
    sent(do_send, do_recv, do_ss, do_rs)
    sent(att_send, att_recv, att_ss, att_rs)
    sent(dq_send, dq_out, dq_ss, dq_rs)
    each(16, lambda i: dkv_copy(i).wait_send())
    for j in range(2):
        remote(core_send.at[j], core_recv.at[j], core_ss.at[j], core_rs.at[j],
               frame=other_core).wait_send()
    for slot, to_x in enumerate((xp, xm, xp, xm, xp, xm)):
        x_copy(slot, to_x).wait_send()
    each(7, lambda i: z_copy(i + 1).wait_send())
    each(7, lambda i: zg_copy(i + 1).wait_send())
    for z in range(8):
        xg_copy(z, 0).wait_send()
        xg_copy(z, 1).wait_send()
        xf_copy(z).wait_send()
    for slot, at in enumerate((x, xm, xp, xo)):
        cg_copy(at, slot).wait_send()


def place_kernel(cam, offs, dq, dkv, gw, gq_hbm, gk_hbm, gv_hbm, gw_hbm, grid, rows, sem):
    c = cam[0]
    off = (offs[(c + 7) % 8, 1], offs[c, 0])
    sel = [selector_t(o) for o in off]
    copies = []
    for n, out in enumerate((gq_hbm, gk_hbm, gv_hbm)):
        for side in range(2):
            for h in range(4):
                unit = side * 4 + h
                if n == 0:
                    placed = dot(sel[side], dq[unit])
                else:
                    unit = (1 - side) * 4 + h
                    placed = dot(sel[side], dkv[0, unit, n - 1]) + dot(sel[side], dkv[1, unit, n - 1])
                grid[n, :, :, side * 32:(side + 1) * 32, h * 128:(h + 1) * 128] = placed.reshape(
                    2, 4, 32, 128)
        copies.append(pltpu.make_async_copy(grid.at[n], out, sem.at[n]))
        copies[-1].start()
    for r in range(8):
        for z in range(8):
            rows[r * 64:(r + 1) * 64, z * 256:(z + 1) * 256] = gw[r // 4, r % 4, z].astype(F32)
        if r % 2:
            part = pl.ds((r - 1) * 64, 128)
            copies.append(pltpu.make_async_copy(rows.at[part], gw_hbm.at[part], sem.at[3 + r // 2]))
            copies[-1].start()
    for copy in copies:
        copy.wait()


def on_device(queries, keys, values, offsets, w_out, grad_out):
    field = queries.shape[1:]
    dma = pltpu.SemaphoreType.DMA
    any_spec = pl.BlockSpec(memory_space=pl.ANY)
    vmem = pl.BlockSpec(memory_space=pltpu.VMEM)
    smem = pl.BlockSpec(memory_space=pltpu.SMEM)
    tile = (128, 128)

    def buf(*shape):
        return pltpu.VMEM(shape, BF)

    layer, dq, dkv, gw = pl.pallas_call(
        main_kernel,
        out_shape=(
            jax.ShapeDtypeStruct((256, 1024), BF),
            jax.ShapeDtypeStruct((8,) + tile, BF),
            jax.ShapeDtypeStruct((2, 8, 2) + tile, BF),
            jax.ShapeDtypeStruct((2, 4, 8, 64, 256), BF),
        ),
        in_specs=[smem] + [any_spec] * 5,
        out_specs=(vmem,) * 4,
        scratch_shapes=[
            buf(*field), buf(*field), buf(*field), buf(512, 2048), buf(2, 256, 1024),
            buf(8, *tile), buf(8, 2, *tile), buf(8, *tile),
            buf(8, *tile), buf(16, 2, *tile), buf(8, *tile),
            buf(128, 2048), buf(128, 2048), buf(4, 2048, 256),
            pltpu.VMEM((4, 128, 256), F32), pltpu.VMEM((4, 1, 256), F32),
            buf(8, *tile), buf(8, *tile), buf(8, *tile),
            pltpu.VMEM((2048, 128), F32), pltpu.VMEM((2048, 128), F32), buf(16, 2, *tile),
            buf(256, 512), buf(512, 256), buf(2, 256, 1024), buf(2, 256, 1024),
            pltpu.VMEM((256, 2048), F32), buf(256, 1024), buf(256, 1024),
            buf(6, 32, 2048), buf(6, 32, 2048), pltpu.VMEM((64, 2048), F32),
            buf(8, 64, 256), buf(8, 64, 256), buf(64, 256), buf(64, 256),
            dma((5,)), dma, dma, dma((8,)), dma((8,)), dma((16,)), dma((16,)), dma((8,)), dma((8,)),
            dma((8,)), dma((8,)), dma((8,)), dma((8,)), dma((16,)), dma((16,)),
            dma((2,)), dma((2,)), dma, dma,
            dma((6,)), dma((6,)), dma((8,)), dma((8,)), dma, dma, dma((8,)), dma((8,)),
            dma((2, 8)), dma((2, 8)), dma((8,)), dma((8,)),
            dma((4,)), dma((4,)),
        ],
        compiler_params=pltpu.CompilerParams(
            collective_id=0, has_side_effects=True, vmem_limit_bytes=56 * 1024 * 1024),
        cost_estimate=pl.CostEstimate(
            flops=5 * 10**9, bytes_accessed=10 * 2**20, transcendentals=2 * 2**20),
        name="strip_attention",
    )(offsets, queries.reshape(field), keys.reshape(field), values.reshape(field), w_out,
      grad_out.reshape(256, 1024))

    grid = jax.ShapeDtypeStruct(field, F32)
    gq, gk, gv, gwo = pl.pallas_call(
        place_kernel,
        out_shape=(grid, grid, grid, jax.ShapeDtypeStruct((512, 2048), F32)),
        in_specs=[smem, smem, vmem, vmem, vmem],
        out_specs=(any_spec,) * 4,
        scratch_shapes=[
            pltpu.VMEM((3,) + field, F32), pltpu.VMEM((512, 2048), F32), dma((7,))],
        compiler_params=pltpu.CompilerParams(vmem_limit_bytes=48 * 1024 * 1024),
        cost_estimate=pl.CostEstimate(
            flops=10**8, bytes_accessed=10 * 2**20, transcendentals=0),
        name="place_gradients",
    )(lax.axis_index("cam").reshape(1), offsets, dq, dkv, gw)
    shape = queries.shape
    return (layer.reshape(grad_out.shape), gq.reshape(shape), gk.reshape(shape), gv.reshape(shape),
            gwo)


def solution(mesh):
    field = P("cam", "frame", None, None, "head")
    rows = P("cam", "frame", None, None, None, "head")
    return jax.shard_map(
        on_device,
        mesh=mesh,
        in_specs=(field, field, field, P(), P("head", None), rows),
        out_specs=(rows, field, field, field, P("head", None)),
        check_vma=False,
    )
```

time: 1680 us -> 123 us (0.07)
  waiting for transfers between devices: 1560 us -> 0 us
  Pallas kernels: 0 us -> 116 us
  local copies, waits for them, and re-layouts: 41.5 us -> 5.91 us
  matrix products: 35.1 us -> 0 us
  between operations: 17.7 us -> 0.68 us
    psum x1 -> x0, waiting for transfers between devices: 1270 us -> none  [on_device(): grad_w_out = lax.psum(local_weight, ('cam', 'frame'))]
    reduce_scatter x2 -> x0, waiting for transfers between devices: 169 us -> none  [the longest x1 147 us: on_device(): lax.psum_scatter(jnp.stack([key_term, value_term], axis=1).reshape(row_co...]
    pallas_call x0 -> x2, Pallas kernels: none -> 116 us  [the longest x1 112 us: on_device(): pl.pallas_call(main_kernel, out_shape=(jax.ShapeDtypeStruct((256, 1024),...]
    all_gather x3 -> x0, waiting for transfers between devices: 107 us -> none  [the longest x1 63.6 us: on_device(): lax.all_gather(near_keys, 'frame', axis=1, tiled=True)]
    dot_general x8 -> x0, matrix products: 26.8 us -> none  [the longest x1 4.87 us: on_device(): jnp.einsum('shqk,skhd->sqhd', weights, value_heads, preferred_element_typ...]
  transfers between devices with their start and end apart: 12 -> 0, of which waited for: 10 -> 0; matrix products, arithmetic and copies ran while one was open for 4% -> 0% of each run, Pallas kernels for 0% -> 0%
where the time goes in v1:
time: 123 us
  Pallas kernels  116 us (94%)
  local copies, waits for them, and re-layouts  5.91 us (5%)
    pallas_call x1, Pallas kernels, on_device(): pl.pallas_call(main_kernel, out_shape=(jax.ShapeDtypeStruct((256, 1024),...  112 us
    unnamed x12, local copies, waits for them, and re-layouts  5.91 us
    pallas_call x1, Pallas kernels, on_device(): pl.pallas_call(place_kernel, out_shape=(grid, grid, grid, jax.ShapeDtypeS...  3.92 us

profile of v1, /device:TPU:1, one launch (start us, length us, event | category | flops | bytes accessed | tf_op | source)
XLA Modules:
  0.0 122.8 jit_solution(854316125695417621)
XLA Ops:
  0.6 1.3 %copy.11.offs = s32[8,2]{1,0:T(8,128)} copy(s32[8,2]{0,1:T(2,128)} %param.9) | data formatting | bytes 128 | tf_op args[3]
  2.0 0.0 copy-start.3
  2.0 112.2 %strip_attention.1 = (bf16[256,1024]{1,0:T(8,128)(2,1)}, bf16[8,128,128]{2,1,0:T(8,128)(2,1)}, bf16[2,8,2,128,128]{4,3,2,1,0:T(8,128)(2,1)}, bf16[2,4,8,64,256]{4,3,2,1,0:T(8,128)(2,1)}) custom-call(s32[8,2]{1,0:T(8,128)} %copy.11.offs, bf16[2,4,64,512]{3,2,1,0:T(8,128)(2,1)} %bitcast.13, bf16[2,4,64,512]{3,2,1,0:T(8,128)(2,1)} %bitcast.14, ...), custom_call_target="tpu_custom_call" | custom-call | flops 5000000000 | bytes 10485760 | tf_op jit(solution)/shard_map/strip_attention/pallas_call | solution.py:420
  114.2 0.0 copy-done.3
  114.2 0.0 copy-start
  114.3 1.6 %copy-done = bf16[2,4,8,64,256]{4,3,2,1,0:T(8,128)(2,1)S(1)} copy-done((bf16[2,4,8,64,256]{4,3,2,1,0:T(8,128)(2,1)S(1)}, bf16[2,4,8,64,256]{4,3,2,1,0:T(8,128)(2,1)}, u32[]{:S(2)}) %copy-start) | copy-done | bytes 2097176
  115.8 0.0 copy-start.1
  115.8 1.2 copy-done.1
  117.1 0.0 copy-start.2
  117.1 0.9 copy-done.2
  118.0 0.0 copy-start.4
  118.0 3.9 %place_gradients.1 = (f32[2,4,64,512]{3,2,1,0:T(8,128)}, f32[2,4,64,512]{3,2,1,0:T(8,128)}, f32[2,4,64,512]{3,2,1,0:T(8,128)}, f32[512,2048]{1,0:T(8,128)}) custom-call(s32[1]{0:T(128)} %bitcast.5.cam, s32[8,2]{1,0:T(8,128)S(1)} %copy-done.3, bf16[8,128,128]{2,1,0:T(8,128)(2,1)S(1)} %copy-done.2, bf16[2,8,2,128,128]{4,3,2,1,0:T(8,128)(2,1)S(1)} %copy-done.1, ...), custom_call_target="tpu_custom_call" | custom-call | flops 100000000 | bytes 10485760 | tf_op jit(solution)/shard_map/place_gradients/pallas_call | solution.py:458
  122.0 0.0 copy-done.4
  122.0 0.8 copy.14
Async XLA Ops:
  2.0 112.3 %copy-start.3 = (s32[8,2]{1,0:T(8,128)S(1)}, s32[8,2]{1,0:T(8,128)}, u32[]{:S(2)}) copy-start(s32[8,2]{1,0:T(8,128)} %copy.11.offs) | copy-start | bytes 196
  114.2 1.6 %copy-start = (bf16[2,4,8,64,256]{4,3,2,1,0:T(8,128)(2,1)S(1)}, bf16[2,4,8,64,256]{4,3,2,1,0:T(8,128)(2,1)}, u32[]{:S(2)}) copy-start(bf16[2,4,8,64,256]{4,3,2,1,0:T(8,128)(2,1)} %get-tuple-element.16.gw) | copy-start | bytes 6291460
  115.8 1.2 copy-start.1
  117.1 0.9 copy-start.2
  118.0 3.9 %copy-start.4 = (bf16[256,1024]{1,0:T(8,128)(2,1)S(1)}, bf16[256,1024]{1,0:T(8,128)(2,1)}, u32[]{:S(2)}) copy-start(bf16[256,1024]{1,0:T(8,128)(2,1)} %get-tuple-element.13) | copy-start | bytes 1572868

commit v2 on v1

v2 whole, which is shorter than its diff:
```python
import functools

import jax
import jax.numpy as jnp
from jax import lax
from jax.experimental import pallas as pl
from jax.experimental.pallas import tpu as pltpu
from jax.sharding import PartitionSpec as P

HD = 128
BF = jnp.bfloat16
F32 = jnp.float32
MESH = pl.DeviceIdType.MESH
LOG2E = 1.4426950408889634
NT = (((1,), (1,)), ((), ()))


def dot(a, b):
    return jnp.dot(a, b, preferred_element_type=F32)


def dot_nt(a, b):
    return lax.dot_general(a, b, NT, preferred_element_type=F32)


def each(count, fn):
    def step(i, carry):
        fn(i)
        return carry

    lax.fori_loop(0, count, step, 0)


def transposed(block):
    return block.astype(F32).T


def selector(off):
    rows = lax.broadcasted_iota(jnp.int32, (128, 256), 0)
    cols = lax.broadcasted_iota(jnp.int32, (128, 256), 1)
    hit = cols == rows + (lax.shift_right_logical(rows, 4) * 16 + off)
    return jnp.where(hit, 1.0, 0.0).astype(BF)


def selector_t(off):
    rows = lax.broadcasted_iota(jnp.int32, (256, 128), 1)
    cols = lax.broadcasted_iota(jnp.int32, (256, 128), 0)
    hit = cols == rows + (lax.shift_right_logical(rows, 4) * 16 + off)
    return jnp.where(hit, 1.0, 0.0).astype(BF)


def main_kernel(
    offs_hbm, q_hbm, k_hbm, v_hbm, w_hbm, g_hbm,
    lo_hbm, dq_hbm, dkv_hbm, gw_hbm,
    offs, q_in, k_in, v_in, w, gfull,
    q_send, kv_send, do_send, q_recv, kv_recv, do_recv,
    kt, vt, probs, o_t, rl,
    att_send, att_recv, dq_send, dq_recv, dk_acc, dv_acc, dkv_send, dkv_recv,
    a_rows, a_t, core_send, core_recv, own, lo_send, lo_recv, lo_done,
    x_send, x_recv, z_send, z_recv, y_send, y_recv, gw,
    in_sem, out_sem, g_ss, g_rs, q_ss, q_rs, kv_ss, kv_rs, do_ss, do_rs,
    att_ss, att_rs, dq_ss, dq_rs, dkv_ss, dkv_rs, core_ss, core_rs, lo_ss, lo_rs,
    x_ss, x_rs, z_ss, z_rs, y_ss, y_rs, zg_ss, zg_rs, xg_ss, xg_rs, cg_ss, cg_rs,
):
    c = lax.axis_index("cam")
    f = lax.axis_index("frame")
    hh = lax.axis_index("head")
    x, yh, k = f // 4, (f // 2) % 2, f % 2
    u = x * 2 + k
    scale = HD ** (-0.5)

    def frame_of(unit):
        return (unit // 2) * 4 + yh * 2 + unit % 2

    def frame_x(to_x):
        return to_x * 4 + yh * 2 + k

    def remote(src, dst, ss, rs, **where):
        return pltpu.make_async_remote_copy(
            src_ref=src, dst_ref=dst, send_sem=ss, recv_sem=rs,
            device_id=where, device_id_type=MESH)

    other_core = x * 4 + yh * 2 + 1 - k
    other_half = x * 4 + (1 - yh) * 2 + k

    barrier = pltpu.get_barrier_semaphore()

    def greet(**where):
        pl.semaphore_signal(barrier, inc=1, device_id=where, device_id_type=MESH)

    def greet_cams(i):
        greet(cam=(c + 1) % 8, frame=i)
        greet(cam=(c + 7) % 8, frame=i)

    loads = [
        pltpu.make_async_copy(src, dst, in_sem.at[i])
        for i, (src, dst) in enumerate(
            ((k_hbm, k_in), (v_hbm, v_in), (q_hbm, q_in), (g_hbm, gfull.at[hh]), (w_hbm, w),
             (offs_hbm, offs)))
    ]
    for load in loads:
        load.start()
    each(16, greet_cams)
    each(7, lambda i: greet(frame=frame_of((u + 1 + i) % 8)))
    each(5, lambda i: greet(cam=(c + 2 + i) % 8))
    greet(frame=other_half)
    greet(head=1 - hh)

    loads[5].wait()
    off = (offs[1, (c + 7) % 8], offs[0, c])
    sel = [selector(o) for o in off]

    def strip(ref, side):
        window = ref[:, :, side * 32:(side + 1) * 32, :].reshape(256, 512)
        return dot(sel[side], window).astype(BF)

    for i, ref in enumerate((k_in, v_in)):
        loads[i].wait()
        for side in range(2):
            cut = strip(ref, side)
            for h in range(4):
                kv_send[h * 2 + 1 - side, i] = cut[:, h * 128:(h + 1) * 128]

    pl.semaphore_wait(barrier, 46)

    def kv_copy(i):
        unit, half = (u + i) % 8, (yh + 1 + i // 8) % 2
        to_cam = (c + 9 - 2 * (unit % 2)) % 8
        to_frame = (unit // 2) * 4 + half * 2 + unit % 2
        return remote(kv_send.at[unit], kv_recv.at[f], kv_ss.at[i], kv_rs.at[f],
                      cam=to_cam, frame=to_frame)

    each(16, lambda i: kv_copy(i).start())

    loads[2].wait()
    for side in range(2):
        cut = strip(q_in, side)
        for h in range(4):
            q_send[h * 2 + side] = cut[:, h * 128:(h + 1) * 128]

    def half_copy(send, recv, ss, rs, i):
        unit = (u + i) % 8
        return remote(send.at[unit], recv.at[u], ss.at[unit], rs.at[u], frame=frame_of(unit))

    def own_copy(send, recv, rs):
        return pltpu.make_async_copy(send.at[u], recv.at[u], rs.at[u])

    own_copy(q_send, q_recv, q_rs).start()
    each(7, lambda i: half_copy(q_send, q_recv, q_ss, q_rs, i + 1).start())
    loads[3].wait()
    g_copy = remote(gfull.at[hh], gfull.at[hh], g_ss, g_rs, head=1 - hh)
    g_copy.start()

    def arrived(ref, sem):
        pltpu.make_async_copy(ref, ref, sem).wait()

    def kv_arrive(i):
        arrived(kv_recv.at[i], kv_rs.at[i])
        cols = pl.ds(pl.multiple_of(i * 128, 128), 128)
        vt[:, cols] = transposed(kv_recv[i, 1]).astype(BF)

    each(16, kv_arrive)

    def send_block(send, recv, ss, rs, unit):
        @pl.when(unit == u)
        def _():
            own_copy(send, recv, rs).start()

        @pl.when(unit != u)
        def _():
            remote(send.at[unit], recv.at[u], ss.at[unit], rs.at[u],
                   frame=frame_of(unit)).start()

    def forward(i):
        b = (x + i) % 4
        for t in range(2):
            arrived(q_recv.at[2 * b + t], q_rs.at[2 * b + t])
        queries = q_recv[pl.ds(2 * b, 2)].reshape(256, 128)
        scores = dot_nt(kv_recv[:, 0].reshape(2048, 128), queries)
        top = jnp.max(scores, axis=0, keepdims=True)
        weights = jnp.exp2((scores - top) * (scale * LOG2E))
        inverse = 1.0 / jnp.sum(weights, axis=0, keepdims=True)
        weights = weights.astype(BF)
        probs[b] = weights
        out_t = dot(vt[...], weights) * inverse
        o_t[b] = out_t
        rl[b] = inverse
        att_send[pl.ds(2 * b, 2)] = out_t.T.astype(BF).reshape(2, 128, 128)
        for t in range(2):
            send_block(att_send, att_recv, att_ss, att_rs, 2 * b + t)

    each(4, forward)

    arrived(gfull.at[1 - hh], g_rs)
    loads[4].wait()
    grad_attn = dot_nt(gfull[0], w[:, :1024]) + dot_nt(gfull[1], w[:, 1024:])
    grad_attn = grad_attn.astype(BF)
    for fr in range(2):
        for s in range(2):
            for h in range(4):
                do_send[h * 2 + s, fr * 64:(fr + 1) * 64] = grad_attn[
                    fr * 128 + s * 64:fr * 128 + s * 64 + 64, h * 128:(h + 1) * 128]
    own_copy(do_send, do_recv, do_rs).start()
    each(7, lambda i: half_copy(do_send, do_recv, do_ss, do_rs, i + 1).start())

    def key_turn(i):
        kt[:, pl.ds(pl.multiple_of(i * 128, 128), 128)] = transposed(kv_recv[i, 0]).astype(BF)

    each(16, key_turn)
    each(8, lambda i: arrived(att_recv.at[i], att_rs.at[i]))
    for fr in range(2):
        for s in range(2):
            for h in range(4):
                a_rows[fr * 128 + s * 64:fr * 128 + s * 64 + 64, h * 128:(h + 1) * 128] = att_recv[
                    h * 2 + s, fr * 64:(fr + 1) * 64]
    for fr in range(2):
        for h in range(4):
            a_t[h * 128:(h + 1) * 128, fr * 128:(fr + 1) * 128] = transposed(
                a_rows[fr * 128:(fr + 1) * 128, h * 128:(h + 1) * 128]).astype(BF)

    theirs = a_t[pl.ds(pl.multiple_of((1 - k) * 256, 256), 256), :]
    for j in range(2):
        core_send[:, j * 1024:(j + 1) * 1024] = dot(theirs, gfull[j]).astype(BF)

    def core_copy(p):
        part = pl.ds(p * 64, 64)
        return remote(core_send.at[part], core_recv.at[part], core_ss.at[p], core_rs.at[p],
                      frame=other_core)

    for p in range(4):
        core_copy(p).start()
    mine = a_t[pl.ds(pl.multiple_of(k * 256, 256), 256), :]
    for j in range(2):
        own[:, j * 1024:(j + 1) * 1024] = dot(mine, gfull[j])

    def x_copy(p, i):
        to = (x + i) % 4
        return remote(x_send.at[p, to], x_recv.at[p, x], x_ss.at[p, i - 1], x_rs.at[p],
                      frame=frame_x(to))

    for p in range(4):
        part = pl.ds(p * 64, 64)
        arrived(core_recv.at[part], core_rs.at[p])
        piece = own[part, :] + core_recv[part, :].astype(F32)
        own[part, :] = piece
        x_send[p] = piece.astype(BF).reshape(4, 16, 2048)
        for i in (1, 3, 2):
            x_copy(p, i).start()

    lo_send[...] = dot(
        a_rows[...], w[:, pl.ds(pl.multiple_of((1 - hh) * 1024, 1024), 1024)]).astype(BF)
    lo_copy = remote(lo_send, lo_recv, lo_ss, lo_rs, head=1 - hh)
    lo_copy.start()

    def backward(i):
        b = (x + i) % 4
        for t in range(2):
            arrived(do_recv.at[2 * b + t], do_rs.at[2 * b + t])
        queries = q_recv[pl.ds(2 * b, 2)].reshape(256, 128)
        weights = probs[b]
        grad_t = transposed(do_recv[pl.ds(2 * b, 2)].reshape(256, 128)) * rl[b]
        delta = jnp.sum(grad_t * o_t[b], axis=0, keepdims=True)
        grads = grad_t.T.astype(BF)
        grad_probs = dot(kv_recv[:, 1].reshape(2048, 128), grad_t.astype(BF))
        grad_scores = (weights.astype(F32) * (grad_probs - delta)).astype(BF)
        grad_q_t = dot(kt[...], grad_scores) * scale
        dq_send[pl.ds(2 * b, 2)] = grad_q_t.T.astype(BF).reshape(2, 128, 128)
        for t in range(2):
            send_block(dq_send, dq_recv, dq_ss, dq_rs, 2 * b + t)
        dk_acc[...] += dot(grad_scores, queries)
        dv_acc[...] += dot(weights, grads)

    dk_acc[...] = jnp.zeros_like(dk_acc)
    dv_acc[...] = jnp.zeros_like(dv_acc)
    each(2, backward)

    def z_copy(p, i):
        to = (c + i) % 8
        return remote(z_send.at[p, to], z_recv.at[p, c], z_ss.at[p], z_rs.at[p], cam=to)

    def x_total(p):
        arrived(x_recv.at[p, pl.ds(0, 3)], x_rs.at[p])
        total = own[pl.ds(pl.multiple_of(p * 64 + x * 16, 16), 16), :]
        for i in range(1, 4):
            total = total + x_recv[p, (x + i) % 4].astype(F32)
        total = total.astype(BF)
        for i in range(8):
            z_send[p, i] = total[:, i * 256:(i + 1) * 256]
        each(7, lambda i: z_copy(p, i + 1).start())

    each(4, x_total)
    backward(2)

    def y_copy(p):
        return remote(y_send.at[p], y_recv.at[p], y_ss.at[p], y_rs.at[p], frame=other_half)

    def z_total(p):
        arrived(z_recv.at[p, pl.ds(0, 7)], z_rs.at[p])
        total = z_send[p, c].astype(F32)
        for i in range(1, 8):
            total = total + z_recv[p, (c + i) % 8].astype(F32)
        y_send[p] = total.astype(BF)
        y_copy(p).start()

    each(4, z_total)
    backward(3)
    dkv_send[:, 0] = (dk_acc[...] * scale).astype(BF).reshape(16, 128, 128)
    dkv_send[:, 1] = dv_acc[...].astype(BF).reshape(16, 128, 128)

    def dkv_copy(i):
        to_frame = (f + i) % 16
        return remote(dkv_send.at[to_frame], dkv_recv.at[yh, u], dkv_ss.at[i],
                      dkv_rs.at[yh * 8 + u], cam=(c + 7 + 2 * k) % 8, frame=to_frame)

    def rows_of(p, to_x):
        return pl.ds(pl.multiple_of(k * 256 + p * 64 + to_x * 16, 16), 16)

    def zg_copy(p, i):
        part = gw.at[rows_of(p, x), pl.ds(pl.multiple_of(c * 256, 256), 256)]
        return remote(part, part, zg_ss.at[p], zg_rs.at[p], cam=(c + i) % 8)

    def total_out(p):
        arrived(y_recv.at[p], y_rs.at[p])
        gw[rows_of(p, x), pl.ds(pl.multiple_of(c * 256, 256), 256)] = (
            y_send[p].astype(F32) + y_recv[p].astype(F32)).astype(BF)
        each(7, lambda i: zg_copy(p, i + 1).start())

    each(4, total_out)
    each(16, lambda i: dkv_copy(i).start())

    here = dot(a_rows[...], w[:, pl.ds(pl.multiple_of(hh * 1024, 1024), 1024)])
    lo_copy.wait()
    lo_done[...] = (here + lo_recv[...].astype(F32)).astype(BF)
    lo_write = pltpu.make_async_copy(lo_done, lo_hbm, out_sem.at[0])
    lo_write.start()

    def xg_copy(p, i):
        part = gw.at[rows_of(p, x), :]
        return remote(part, part, xg_ss.at[p], xg_rs.at[p], frame=frame_x((x + i) % 4))

    def z_gathered(p):
        arrived(z_recv.at[p, pl.ds(0, 7)], zg_rs.at[p])
        for i in (1, 3, 2):
            xg_copy(p, i).start()

    each(4, z_gathered)

    def core_rows(p, core):
        return gw.at[pl.ds(pl.multiple_of(core * 256 + p * 64, 64), 64), :]

    def cg_copy(p):
        return remote(core_rows(p, k), core_rows(p, k), cg_ss.at[p], cg_rs.at[p], frame=other_core)

    def gw_write(p, core):
        at = pl.ds(pl.multiple_of(core * 256 + p * 64, 64), 64)
        return pltpu.make_async_copy(gw.at[at], gw_hbm.at[at], out_sem.at[3 + p * 2 + core])

    def x_gathered(p):
        arrived(x_recv.at[p, pl.ds(0, 3)], xg_rs.at[p])
        cg_copy(p).start()
        gw_write(p, k).start()

    each(4, x_gathered)

    each(8, lambda i: arrived(dq_recv.at[i], dq_rs.at[i]))
    dq_write = pltpu.make_async_copy(dq_recv, dq_hbm, out_sem.at[1])
    dq_write.start()
    each(16, lambda i: arrived(dkv_recv.at[i // 8, i % 8], dkv_rs.at[i]))
    dkv_write = pltpu.make_async_copy(dkv_recv, dkv_hbm, out_sem.at[2])
    dkv_write.start()

    def core_gathered(p):
        arrived(core_rows(p, 1 - k), cg_rs.at[p])
        gw_write(p, 1 - k).start()

    each(4, core_gathered)

    g_copy.wait_send()
    each(16, lambda i: kv_copy(i).wait_send())

    def sent(send, recv, ss, rs):
        each(7, lambda i: half_copy(send, recv, ss, rs, i + 1).wait_send())

    sent(q_send, q_recv, q_ss, q_rs)
    sent(do_send, do_recv, do_ss, do_rs)
    sent(att_send, att_recv, att_ss, att_rs)
    sent(dq_send, dq_recv, dq_ss, dq_rs)
    each(16, lambda i: dkv_copy(i).wait_send())

    def pieces_sent(p):
        core_copy(p).wait_send()
        for i in (1, 2, 3):
            x_copy(p, i).wait_send()
        arrived(z_recv.at[p, pl.ds(0, 7)], z_ss.at[p])
        y_copy(p).wait_send()
        arrived(z_recv.at[p, pl.ds(0, 7)], zg_ss.at[p])
        arrived(x_recv.at[p, pl.ds(0, 3)], xg_ss.at[p])
        cg_copy(p).wait_send()
        gw_write(p, k).wait()
        gw_write(p, 1 - k).wait()

    each(4, pieces_sent)
    lo_write.wait()
    dq_write.wait()
    dkv_write.wait()


def place_kernel(
    offs_hbm, lo_hbm, dq_hbm, dkv_hbm, gw_hbm, layer_hbm, gq_hbm, gk_hbm, gv_hbm, gwo_hbm,
    offs, dq, dkv, gw, lo, grid, rows, in_sem, out_sem,
):
    c = lax.axis_index("cam")
    loads = [pltpu.make_async_copy(offs_hbm, offs, in_sem.at[0]),
             pltpu.make_async_copy(dq_hbm, dq, in_sem.at[1]),
             pltpu.make_async_copy(dkv_hbm, dkv, in_sem.at[2]),
             pltpu.make_async_copy(lo_hbm, lo, in_sem.at[3])]
    part = [pl.ds(r * 128, 128) for r in range(4)]
    loads += [pltpu.make_async_copy(gw_hbm.at[part[r]], gw.at[part[r]], in_sem.at[4 + r])
              for r in range(4)]
    for load in loads:
        load.start()
    loads[0].wait()
    off = (offs[1, (c + 7) % 8], offs[0, c])
    sel = [selector_t(o) for o in off]
    writes = []

    def write(src, dst):
        writes.append(pltpu.make_async_copy(src, dst, out_sem.at[len(writes)]))
        writes[-1].start()

    for n, out in enumerate((gq_hbm, gk_hbm, gv_hbm)):
        if n < 2:
            loads[1 + n].wait()
        for side in range(2):
            for h in range(4):
                unit = h * 2 + (side if n == 0 else 1 - side)
                if n == 0:
                    placed = dot(sel[side], dq[unit])
                else:
                    placed = dot(sel[side], dkv[0, unit, n - 1]) + dot(sel[side], dkv[1, unit, n - 1])
                grid[n, :, :, side * 32:(side + 1) * 32, h * 128:(h + 1) * 128] = placed.reshape(
                    2, 4, 32, 128)
        write(grid.at[n], out)
    loads[3].wait()
    write(lo, layer_hbm)
    for r in range(4):
        loads[4 + r].wait()
        rows[part[r], :] = gw[part[r], :].astype(F32)
        write(rows.at[part[r]], gwo_hbm.at[part[r]])
    for copy in writes:
        copy.wait()


def on_device(queries, keys, values, offsets, w_out, grad_out):
    field = queries.shape[1:]
    dma = pltpu.SemaphoreType.DMA
    any_spec = pl.BlockSpec(memory_space=pl.ANY)
    tile = (128, 128)

    def buf(*shape):
        return pltpu.VMEM(shape, BF)

    mid = [
        jax.ShapeDtypeStruct((256, 1024), BF),
        jax.ShapeDtypeStruct((8,) + tile, BF),
        jax.ShapeDtypeStruct((2, 8, 2) + tile, BF),
        jax.ShapeDtypeStruct((512, 2048), BF),
    ]
    offs = offsets.T
    parts = pl.pallas_call(
        main_kernel,
        out_shape=mid,
        in_specs=[any_spec] * 6,
        out_specs=[any_spec] * 4,
        scratch_shapes=[
            pltpu.SMEM((2, 8), jnp.int32),
            buf(*field), buf(*field), buf(*field), buf(512, 2048), buf(2, 256, 1024),
            buf(8, *tile), buf(8, 2, *tile), buf(8, *tile),
            buf(8, *tile), buf(16, 2, *tile), buf(8, *tile),
            buf(128, 2048), buf(128, 2048), buf(4, 2048, 256),
            pltpu.VMEM((4, 128, 256), F32), pltpu.VMEM((4, 1, 256), F32),
            buf(8, *tile), buf(8, *tile), buf(8, *tile), buf(8, *tile),
            pltpu.VMEM((2048, 128), F32), pltpu.VMEM((2048, 128), F32),
            buf(16, 2, *tile), buf(2, 8, 2, *tile),
            buf(256, 512), buf(512, 256), buf(256, 2048), buf(256, 2048),
            pltpu.VMEM((256, 2048), F32), buf(256, 1024), buf(256, 1024), buf(256, 1024),
            buf(4, 4, 16, 2048), buf(4, 4, 16, 2048),
            buf(4, 8, 16, 256), buf(4, 8, 16, 256), buf(4, 16, 256), buf(4, 16, 256),
            buf(512, 2048),
            dma((6,)), dma((11,)), dma, dma, dma((8,)), dma((8,)), dma((16,)), dma((16,)),
            dma((8,)), dma((8,)),
            dma((8,)), dma((8,)), dma((8,)), dma((8,)), dma((16,)), dma((16,)),
            dma((4,)), dma((4,)), dma, dma,
            dma((4, 3)), dma((4,)), dma((4,)), dma((4,)), dma((4,)), dma((4,)),
            dma((4,)), dma((4,)), dma((4,)), dma((4,)), dma((4,)), dma((4,)),
        ],
        compiler_params=pltpu.CompilerParams(
            collective_id=0, has_side_effects=True, vmem_limit_bytes=56 * 1024 * 1024),
        cost_estimate=pl.CostEstimate(
            flops=5 * 10**9, bytes_accessed=10 * 2**20, transcendentals=2 * 2**20),
        name="strip_attention",
    )(offs, queries.reshape(field), keys.reshape(field), values.reshape(field), w_out,
      grad_out.reshape(256, 1024))

    grid = jax.ShapeDtypeStruct(field, F32)
    layer, gq, gk, gv, gwo = pl.pallas_call(
        place_kernel,
        out_shape=(mid[0], grid, grid, grid, jax.ShapeDtypeStruct((512, 2048), F32)),
        in_specs=[any_spec] * 5,
        out_specs=(any_spec,) * 5,
        scratch_shapes=[
            pltpu.SMEM((2, 8), jnp.int32), buf(8, *tile), buf(2, 8, 2, *tile), buf(512, 2048),
            buf(256, 1024), pltpu.VMEM((3,) + field, F32), pltpu.VMEM((512, 2048), F32),
            dma((8,)), dma((8,))],
        compiler_params=pltpu.CompilerParams(vmem_limit_bytes=60 * 1024 * 1024),
        cost_estimate=pl.CostEstimate(
            flops=10**8, bytes_accessed=10 * 2**20, transcendentals=0),
        name="place_gradients",
    )(offs, *parts)
    shape = queries.shape
    return (layer.reshape(grad_out.shape), gq.reshape(shape), gk.reshape(shape), gv.reshape(shape),
            gwo)


def solution(mesh):
    field = P("cam", "frame", None, None, "head")
    rows = P("cam", "frame", None, None, None, "head")
    return jax.shard_map(
        on_device,
        mesh=mesh,
        in_specs=(field, field, field, P(), P("head", None), rows),
        out_specs=(rows, field, field, field, P("head", None)),
        check_vma=False,
    )
```

time: 123 us -> 99.1 us (0.81)
  Pallas kernels: 116 us -> 98.3 us
  local copies, waits for them, and re-layouts: 5.91 us -> 0 us
    pallas_call x2, Pallas kernels: 116 us -> 98.3 us  [the longest x1 93.6 us: on_device(): pl.pallas_call(main_kernel, out_shape=mid, in_specs=[any_spec] * 6, out_s...]
    unnamed x12 -> x0, local copies, waits for them, and re-layouts: 5.91 us -> none
where the time goes in v2:
time: 99.1 us; the launch traced here: 99 us
  Pallas kernels  98.3 us (99%)
    pallas_call x1, Pallas kernels, on_device(): pl.pallas_call(main_kernel, out_shape=mid, in_specs=[any_spec] * 6, out_s...  93.6 us
    pallas_call x1, Pallas kernels, on_device(): pl.pallas_call(place_kernel, out_shape=(mid[0], grid, grid, grid, jax.Sha...  4.69 us

profile of v2, /device:TPU:1, one launch (start us, length us, event | category | flops | bytes accessed | tf_op | source)
XLA Modules:
  0.0 99.0 jit_solution(13690863877126332722)
XLA Ops:
  0.6 93.6 %strip_attention.1 = (bf16[256,1024]{1,0:T(8,128)(2,1)}, bf16[8,128,128]{2,1,0:T(8,128)(2,1)}, bf16[2,8,2,128,128]{4,3,2,1,0:T(8,128)(2,1)}, bf16[512,2048]{1,0:T(8,128)(2,1)}) custom-call(s32[2,8]{1,0:T(2,128)} %bitcast.9, bf16[2,4,64,512]{3,2,1,0:T(8,128)(2,1)} %bitcast.14, bf16[2,4,64,512]{3,2,1,0:T(8,128)(2,1)} %bitcast.15, ...), custom_call_target="tpu_custom_call" | custom-call | flops 5000000000 | bytes 10485760 | tf_op jit(solution)/shard_map/strip_attention/pallas_call | solution.py:470
  94.3 4.7 %place_gradients.1 = (bf16[256,1024]{1,0:T(8,128)(2,1)}, f32[2,4,64,512]{3,2,1,0:T(8,128)}, f32[2,4,64,512]{3,2,1,0:T(8,128)}, f32[2,4,64,512]{3,2,1,0:T(8,128)}, f32[512,2048]{1,0:T(8,128)}) custom-call(s32[2,8]{1,0:T(2,128)} %bitcast.10, bf16[256,1024]{1,0:T(8,128)(2,1)} %get-tuple-element.14.lo_hbm, bf16[8,128,128]{2,1,0:T(8,128)(2,1)} %get-tuple-element.15.dq_hbm, ...), custom_call_target="tpu_custom_call" | custom-call | flops 100000000 | bytes 10485760 | tf_op jit(solution)/shard_map/place_gradients/pallas_call | solution.py:506

commit v3 on v2

v3 whole, which is shorter than its diff:
```python
import functools

import jax
import jax.numpy as jnp
from jax import lax
from jax.experimental import pallas as pl
from jax.experimental.pallas import tpu as pltpu
from jax.sharding import PartitionSpec as P

HD = 128
BF = jnp.bfloat16
F32 = jnp.float32
MESH = pl.DeviceIdType.MESH
LOG2E = 1.4426950408889634
NT = (((1,), (1,)), ((), ()))


def dot(a, b):
    return jnp.dot(a, b, preferred_element_type=F32)


def dot_nt(a, b):
    return lax.dot_general(a, b, NT, preferred_element_type=F32)


def each(count, fn):
    def step(i, carry):
        fn(i)
        return carry

    lax.fori_loop(0, count, step, 0)


def transposed(block):
    return block.astype(F32).T


def selector(off):
    rows = lax.broadcasted_iota(jnp.int32, (128, 256), 0)
    cols = lax.broadcasted_iota(jnp.int32, (128, 256), 1)
    hit = cols == rows + (lax.shift_right_logical(rows, 4) * 16 + off)
    return jnp.where(hit, 1.0, 0.0).astype(BF)


def selector_t(off):
    rows = lax.broadcasted_iota(jnp.int32, (256, 128), 1)
    cols = lax.broadcasted_iota(jnp.int32, (256, 128), 0)
    hit = cols == rows + (lax.shift_right_logical(rows, 4) * 16 + off)
    return jnp.where(hit, 1.0, 0.0).astype(BF)


def main_kernel(
    offs_hbm, q_hbm, k_hbm, v_hbm, w_hbm, g_hbm,
    lo_hbm, dq_hbm, dkv_hbm, gw_hbm,
    offs, q_in, k_in, v_in, w, gfull,
    q_send, kv_send, do_send, q_recv, kv_recv, do_recv,
    kt, vt, probs, o_t, rl,
    att_send, att_recv, dq_acc, dq_send, dq_recv, dk_acc, dv_acc, far_send, far_recv, dkv_send, dkv_recv,
    a_rows, a_t, core_send, core_recv, own, lo_send, lo_recv, lo_done,
    x_send, x_recv, z_send, z_recv, y_send, y_recv, gw,
    in_sem, out_sem, g_ss, g_rs, q_ss, q_rs, kv_ss, kv_rs, do_ss, do_rs,
    att_ss, att_rs, dq_ss, dq_rs, far_ss, far_rs, dkv_ss, dkv_rs, core_ss, core_rs, lo_ss, lo_rs,
    x_ss, x_rs, z_ss, z_rs, y_ss, y_rs, zg_ss, zg_rs, xg_ss, xg_rs, cg_ss, cg_rs,
):
    c = lax.axis_index("cam")
    f = lax.axis_index("frame")
    hh = lax.axis_index("head")
    x, yh, k = f // 4, (f // 2) % 2, f % 2
    u = x * 2 + k
    scale = HD ** (-0.5)

    def frame_of(unit):
        return (unit // 2) * 4 + yh * 2 + unit % 2

    def frame_x(to_x):
        return to_x * 4 + yh * 2 + k

    def remote(src, dst, ss, rs, **where):
        return pltpu.make_async_remote_copy(
            src_ref=src, dst_ref=dst, send_sem=ss, recv_sem=rs,
            device_id=where, device_id_type=MESH)

    other_core = x * 4 + yh * 2 + 1 - k
    other_half = x * 4 + (1 - yh) * 2 + k

    barrier = pltpu.get_barrier_semaphore()

    def greet(**where):
        pl.semaphore_signal(barrier, inc=1, device_id=where, device_id_type=MESH)

    def greet_cams(i):
        greet(cam=(c + 1) % 8, frame=i)
        greet(cam=(c + 7) % 8, frame=i)

    loads = [
        pltpu.make_async_copy(src, dst, in_sem.at[i])
        for i, (src, dst) in enumerate(
            ((k_hbm, k_in), (v_hbm, v_in), (q_hbm, q_in), (g_hbm, gfull.at[hh]), (w_hbm, w),
             (offs_hbm, offs)))
    ]
    for load in loads:
        load.start()
    each(16, greet_cams)
    each(7, lambda i: greet(frame=frame_of((u + 1 + i) % 8)))
    each(5, lambda i: greet(cam=(c + 2 + i) % 8))
    greet(frame=other_half)
    greet(head=1 - hh)

    loads[5].wait()
    off = (offs[1, (c + 7) % 8], offs[0, c])
    sel = [selector(o) for o in off]

    def strip(ref, side):
        window = ref[:, :, side * 32:(side + 1) * 32, :].reshape(256, 512)
        return dot(sel[side], window).astype(BF)

    for i, ref in enumerate((k_in, v_in)):
        loads[i].wait()
        for side in range(2):
            cut = strip(ref, side)
            for h in range(4):
                kv_send[h * 2 + 1 - side, i] = cut[:, h * 128:(h + 1) * 128]

    pl.semaphore_wait(barrier, 46)

    def kv_copy(i):
        unit, half = (u + i) % 8, (yh + 1 + i // 8) % 2
        to_cam = (c + 9 - 2 * (unit % 2)) % 8
        to_frame = (unit // 2) * 4 + half * 2 + unit % 2
        return remote(kv_send.at[unit], kv_recv.at[yh, u], kv_ss.at[i], kv_rs.at[yh * 8 + u],
                      cam=to_cam, frame=to_frame)

    each(16, lambda i: kv_copy(i).start())

    loads[2].wait()
    for side in range(2):
        cut = strip(q_in, side)
        for h in range(4):
            q_send[h * 2 + side] = cut[:, h * 128:(h + 1) * 128]

    def half_copy(send, recv, ss, rs, i):
        unit = (u + i) % 8
        return remote(send.at[unit], recv.at[u], ss.at[unit], rs.at[u], frame=frame_of(unit))

    def own_copy(send, recv, rs):
        return pltpu.make_async_copy(send.at[u], recv.at[u], rs.at[u])

    own_copy(q_send, q_recv, q_rs).start()
    each(7, lambda i: half_copy(q_send, q_recv, q_ss, q_rs, i + 1).start())
    loads[3].wait()
    g_copy = remote(gfull.at[hh], gfull.at[hh], g_ss, g_rs, head=1 - hh)
    g_copy.start()

    def arrived(ref, sem):
        pltpu.make_async_copy(ref, ref, sem).wait()

    def kv_arrive(i):
        half, source = i // 8, i % 8
        arrived(kv_recv.at[half, source], kv_rs.at[i])
        cols = pl.ds(pl.multiple_of(source * 128, 128), 128)
        vt[half, :, cols] = transposed(kv_recv[half, source, 1]).astype(BF)

    each(16, kv_arrive)

    def stacked(half, i):
        return kv_recv[half, :, i].reshape(1024, 128)

    def send_block(send, recv, ss, rs, unit):
        @pl.when(unit == u)
        def _():
            own_copy(send, recv, rs).start()

        @pl.when(unit != u)
        def _():
            remote(send.at[unit], recv.at[u], ss.at[unit], rs.at[u],
                   frame=frame_of(unit)).start()

    def forward(i):
        b = (x + i) % 4
        for t in range(2):
            arrived(q_recv.at[2 * b + t], q_rs.at[2 * b + t])
        queries = q_recv[pl.ds(2 * b, 2)].reshape(256, 128)
        scores = [dot_nt(stacked(half, 0), queries) for half in range(2)]
        top = jnp.maximum(jnp.max(scores[0], axis=0, keepdims=True),
                          jnp.max(scores[1], axis=0, keepdims=True))
        total, out_t = 0.0, 0.0
        for half in range(2):
            weights = jnp.exp2((scores[half] - top) * (scale * LOG2E))
            total = total + jnp.sum(weights, axis=0, keepdims=True)
            weights = weights.astype(BF)
            probs[half, b] = weights
            out_t = out_t + dot(vt[half], weights)
        inverse = 1.0 / total
        out_t = out_t * inverse
        o_t[b] = out_t
        rl[b] = inverse
        att_send[pl.ds(2 * b, 2)] = out_t.T.astype(BF).reshape(2, 128, 128)
        for t in range(2):
            send_block(att_send, att_recv, att_ss, att_rs, 2 * b + t)

    each(4, forward)

    each(8, lambda i: arrived(att_recv.at[i], att_rs.at[i]))
    for fr in range(2):
        for s in range(2):
            for h in range(4):
                a_rows[fr * 128 + s * 64:fr * 128 + s * 64 + 64, h * 128:(h + 1) * 128] = att_recv[
                    h * 2 + s, fr * 64:(fr + 1) * 64]
    for fr in range(2):
        for h in range(4):
            a_t[h * 128:(h + 1) * 128, fr * 128:(fr + 1) * 128] = transposed(
                a_rows[fr * 128:(fr + 1) * 128, h * 128:(h + 1) * 128]).astype(BF)

    features = (hh, 1 - hh)

    def core_copy(p):
        part = (p // 2, pl.ds(p % 2 * 128, 128))
        return remote(core_send.at[part], core_recv.at[part], core_ss.at[p], core_rs.at[p],
                      frame=other_core)

    def multiply(g):
        theirs = a_t[pl.ds(pl.multiple_of((1 - k) * 256, 256), 256), :]
        core_send[g] = dot(theirs, gfull[features[g]]).astype(BF)
        core_copy(2 * g).start()
        core_copy(2 * g + 1).start()
        mine = a_t[pl.ds(pl.multiple_of(k * 256, 256), 256), :]
        own[g] = dot(mine, gfull[features[g]])

    def x_copy(p, i):
        to = (x + i) % 4
        return remote(x_send.at[p, to], x_recv.at[p, x], x_ss.at[p, i - 1], x_rs.at[p],
                      frame=frame_x(to))

    def core_total(p):
        part = pl.ds(p % 2 * 128, 128)
        arrived(core_recv.at[p // 2, part], core_rs.at[p])
        piece = own[p // 2, part, :] + core_recv[p // 2, part, :].astype(F32)
        own[p // 2, part, :] = piece
        x_send[p] = piece.astype(BF).reshape(4, 32, 1024)
        for i in (1, 3, 2):
            x_copy(p, i).start()

    def z_copy(p, i):
        to = (c + i) % 8
        return remote(z_send.at[p, to], z_recv.at[p, c], z_ss.at[p], z_rs.at[p], cam=to)

    def x_total(p):
        arrived(x_recv.at[p, pl.ds(0, 3)], x_rs.at[p])
        total = own[p // 2, pl.ds(pl.multiple_of(p % 2 * 128 + x * 32, 32), 32), :]
        for i in range(1, 4):
            total = total + x_recv[p, (x + i) % 4].astype(F32)
        total = total.astype(BF)
        for i in range(8):
            z_send[p, i] = total[:, i * 128:(i + 1) * 128]
        each(7, lambda i: z_copy(p, i + 1).start())

    def y_copy(p):
        return remote(y_send.at[p], y_recv.at[p], y_ss.at[p], y_rs.at[p], frame=other_half)

    def z_total(p):
        arrived(z_recv.at[p, pl.ds(0, 7)], z_rs.at[p])
        total = z_send[p, c].astype(F32)
        for i in range(1, 8):
            total = total + z_recv[p, (c + i) % 8].astype(F32)
        y_send[p] = total.astype(BF)
        y_copy(p).start()

    def piece_at(p, core, to_x=None, z=None):
        row, rows = core * 256 + p % 2 * 128, 128
        if to_x is not None:
            row, rows = row + to_x * 32, 32
        col, cols = features[p // 2] * 1024, 1024
        if z is not None:
            col, cols = col + z * 128, 128
        return (pl.ds(pl.multiple_of(row, rows), rows), pl.ds(pl.multiple_of(col, cols), cols))

    def zg_copy(p, i):
        part = gw.at[piece_at(p, k, x, c)]
        return remote(part, part, zg_ss.at[p], zg_rs.at[p], cam=(c + i) % 8)

    def y_total(p):
        arrived(y_recv.at[p], y_rs.at[p])
        rows, cols = piece_at(p, k, x, c)
        gw[rows, cols] = (y_send[p].astype(F32) + y_recv[p].astype(F32)).astype(BF)
        each(7, lambda i: zg_copy(p, i + 1).start())

    def xg_copy(p, i):
        part = gw.at[piece_at(p, k, x)]
        return remote(part, part, xg_ss.at[p], xg_rs.at[p], frame=frame_x((x + i) % 4))

    def z_gathered(p):
        arrived(z_recv.at[p, pl.ds(0, 7)], zg_rs.at[p])
        for i in (1, 3, 2):
            xg_copy(p, i).start()

    def cg_copy(p):
        part = gw.at[piece_at(p, k)]
        return remote(part, part, cg_ss.at[p], cg_rs.at[p], frame=other_core)

    def gw_write(p, core):
        at = piece_at(p, core)
        return pltpu.make_async_copy(gw.at[at], gw_hbm.at[at], out_sem.at[3 + p * 2 + core])

    def x_gathered(p):
        arrived(x_recv.at[p, pl.ds(0, 3)], xg_rs.at[p])
        cg_copy(p).start()
        gw_write(p, k).start()

    def core_gathered(p):
        arrived(gw.at[piece_at(p, 1 - k)], cg_rs.at[p])
        gw_write(p, 1 - k).start()

    def backward(half, i):
        b = (x + i) % 4
        if half is far:
            for t in range(2):
                arrived(do_recv.at[2 * b + t], do_rs.at[2 * b + t])
        queries = q_recv[pl.ds(2 * b, 2)].reshape(256, 128)
        weights = probs[half, b]
        grad_t = transposed(do_recv[pl.ds(2 * b, 2)].reshape(256, 128)) * rl[b]
        delta = jnp.sum(grad_t * o_t[b], axis=0, keepdims=True)
        grads = grad_t.T.astype(BF)
        grad_probs = dot(stacked(half, 1), grad_t.astype(BF))
        grad_scores = (weights.astype(F32) * (grad_probs - delta)).astype(BF)
        grad_q_t = dot(kt[half], grad_scores)
        if half is far:
            dq_acc[b] = grad_q_t
        else:
            grad_q_t = (grad_q_t + dq_acc[b]) * scale
            dq_send[pl.ds(2 * b, 2)] = grad_q_t.T.astype(BF).reshape(2, 128, 128)
            for t in range(2):
                send_block(dq_send, dq_recv, dq_ss, dq_rs, 2 * b + t)
        if i == 0:
            dk_acc[...] = dot(grad_scores, queries)
            dv_acc[...] = dot(weights, grads)
        else:
            dk_acc[...] += dot(grad_scores, queries)
            dv_acc[...] += dot(weights, grads)

    def far_copy():
        return remote(far_send, far_recv, far_ss, far_rs, frame=other_half)

    def dkv_copy(i):
        source = (u + i) % 8
        return remote(dkv_send.at[source], dkv_recv.at[u], dkv_ss.at[i], dkv_rs.at[u],
                      cam=(c + 7 + 2 * k) % 8, frame=frame_of(source))

    far, near = 1 - yh, yh

    multiply(0)

    def key_turn(i):
        half, source = i // 8, i % 8
        kt[half, :, pl.ds(pl.multiple_of(source * 128, 128), 128)] = transposed(
            kv_recv[half, source, 0]).astype(BF)

    core_total(0)
    core_total(1)
    each(16, key_turn)
    arrived(gfull.at[1 - hh], g_rs)
    loads[4].wait()
    grad_attn = dot_nt(gfull[0], w[:, :1024]) + dot_nt(gfull[1], w[:, 1024:])
    grad_attn = grad_attn.astype(BF)
    for fr in range(2):
        for s in range(2):
            for h in range(4):
                do_send[h * 2 + s, fr * 64:(fr + 1) * 64] = grad_attn[
                    fr * 128 + s * 64:fr * 128 + s * 64 + 64, h * 128:(h + 1) * 128]
    own_copy(do_send, do_recv, do_rs).start()
    each(7, lambda i: half_copy(do_send, do_recv, do_ss, do_rs, i + 1).start())
    multiply(1)
    x_total(0)
    x_total(1)
    lo_send[...] = dot(
        a_rows[...], w[:, pl.ds(pl.multiple_of((1 - hh) * 1024, 1024), 1024)]).astype(BF)
    lo_copy = remote(lo_send, lo_recv, lo_ss, lo_rs, head=1 - hh)
    lo_copy.start()
    core_total(2)
    core_total(3)
    backward(far, 0)
    backward(far, 1)
    z_total(0)
    z_total(1)
    backward(far, 2)
    backward(far, 3)
    far_send[:, 0] = dk_acc[...].astype(BF).reshape(8, 128, 128)
    far_send[:, 1] = dv_acc[...].astype(BF).reshape(8, 128, 128)
    far_copy().start()
    x_total(2)
    x_total(3)
    y_total(0)
    y_total(1)
    backward(near, 0)
    backward(near, 1)
    z_total(2)
    z_total(3)
    z_gathered(0)
    z_gathered(1)
    backward(near, 2)
    backward(near, 3)
    y_total(2)
    y_total(3)
    x_gathered(0)
    x_gathered(1)
    far_copy().wait()
    for i, acc in enumerate((dk_acc, dv_acc)):
        total = acc[...].reshape(8, 128, 128) + far_recv[:, i].astype(F32)
        if i == 0:
            total = total * scale
        dkv_send[:, i] = total.astype(BF)
    each(8, lambda i: dkv_copy(i).start())
    z_gathered(2)
    z_gathered(3)

    here = dot(a_rows[...], w[:, pl.ds(pl.multiple_of(hh * 1024, 1024), 1024)])
    lo_copy.wait()
    lo_done[...] = (here + lo_recv[...].astype(F32)).astype(BF)
    lo_write = pltpu.make_async_copy(lo_done, lo_hbm, out_sem.at[0])
    lo_write.start()

    core_gathered(0)
    core_gathered(1)
    each(8, lambda i: arrived(dq_recv.at[i], dq_rs.at[i]))
    dq_write = pltpu.make_async_copy(dq_recv, dq_hbm, out_sem.at[1])
    dq_write.start()
    each(8, lambda i: arrived(dkv_recv.at[i], dkv_rs.at[i]))
    dkv_write = pltpu.make_async_copy(dkv_recv, dkv_hbm, out_sem.at[2])
    dkv_write.start()
    x_gathered(2)
    x_gathered(3)
    core_gathered(2)
    core_gathered(3)

    g_copy.wait_send()
    each(16, lambda i: kv_copy(i).wait_send())

    def sent(send, recv, ss, rs):
        each(7, lambda i: half_copy(send, recv, ss, rs, i + 1).wait_send())

    sent(q_send, q_recv, q_ss, q_rs)
    sent(do_send, do_recv, do_ss, do_rs)
    sent(att_send, att_recv, att_ss, att_rs)
    sent(dq_send, dq_recv, dq_ss, dq_rs)
    each(8, lambda i: dkv_copy(i).wait_send())
    for p in range(4):
        core_copy(p).wait_send()
        for i in (1, 2, 3):
            x_copy(p, i).wait_send()
        arrived(z_recv.at[p, pl.ds(0, 7)], z_ss.at[p])
        y_copy(p).wait_send()
        arrived(z_recv.at[p, pl.ds(0, 7)], zg_ss.at[p])
        arrived(x_recv.at[p, pl.ds(0, 3)], xg_ss.at[p])
        cg_copy(p).wait_send()
        gw_write(p, k).wait()
        gw_write(p, 1 - k).wait()
    lo_write.wait()
    dq_write.wait()
    dkv_write.wait()


def place_kernel(
    offs_hbm, lo_hbm, dq_hbm, dkv_hbm, gw_hbm, layer_hbm, gq_hbm, gk_hbm, gv_hbm, gwo_hbm,
    offs, dq, dkv, gw, lo, grid, rows, in_sem, out_sem,
):
    c = lax.axis_index("cam")
    loads = [pltpu.make_async_copy(offs_hbm, offs, in_sem.at[0]),
             pltpu.make_async_copy(dq_hbm, dq, in_sem.at[1]),
             pltpu.make_async_copy(dkv_hbm, dkv, in_sem.at[2]),
             pltpu.make_async_copy(lo_hbm, lo, in_sem.at[3])]
    part = [pl.ds(r * 128, 128) for r in range(4)]
    loads += [pltpu.make_async_copy(gw_hbm.at[part[r]], gw.at[part[r]], in_sem.at[4 + r])
              for r in range(4)]
    for load in loads:
        load.start()
    loads[0].wait()
    off = (offs[1, (c + 7) % 8], offs[0, c])
    sel = [selector_t(o) for o in off]
    writes = []

    def write(src, dst):
        writes.append(pltpu.make_async_copy(src, dst, out_sem.at[len(writes)]))
        writes[-1].start()

    for n, out in enumerate((gq_hbm, gk_hbm, gv_hbm)):
        if n < 2:
            loads[1 + n].wait()
        for side in range(2):
            for h in range(4):
                unit = h * 2 + (side if n == 0 else 1 - side)
                if n == 0:
                    placed = dot(sel[side], dq[unit])
                else:
                    placed = dot(sel[side], dkv[unit, n - 1])
                grid[n, :, :, side * 32:(side + 1) * 32, h * 128:(h + 1) * 128] = placed.reshape(
                    2, 4, 32, 128)
        write(grid.at[n], out)
    loads[3].wait()
    write(lo, layer_hbm)
    for r in range(4):
        loads[4 + r].wait()
        rows[part[r], :] = gw[part[r], :].astype(F32)
        write(rows.at[part[r]], gwo_hbm.at[part[r]])
    for copy in writes:
        copy.wait()


def on_device(queries, keys, values, offsets, w_out, grad_out):
    field = queries.shape[1:]
    dma = pltpu.SemaphoreType.DMA
    any_spec = pl.BlockSpec(memory_space=pl.ANY)
    tile = (128, 128)

    def buf(*shape):
        return pltpu.VMEM(shape, BF)

    mid = [
        jax.ShapeDtypeStruct((256, 1024), BF),
        jax.ShapeDtypeStruct((8,) + tile, BF),
        jax.ShapeDtypeStruct((8, 2) + tile, BF),
        jax.ShapeDtypeStruct((512, 2048), BF),
    ]
    offs = offsets.T
    parts = pl.pallas_call(
        main_kernel,
        out_shape=mid,
        in_specs=[any_spec] * 6,
        out_specs=[any_spec] * 4,
        scratch_shapes=[
            pltpu.SMEM((2, 8), jnp.int32),
            buf(*field), buf(*field), buf(*field), buf(512, 2048), buf(2, 256, 1024),
            buf(8, *tile), buf(8, 2, *tile), buf(8, *tile),
            buf(8, *tile), buf(2, 8, 2, *tile), buf(8, *tile),
            buf(2, 128, 1024), buf(2, 128, 1024), buf(2, 4, 1024, 256),
            pltpu.VMEM((4, 128, 256), F32), pltpu.VMEM((4, 1, 256), F32),
            buf(8, *tile), buf(8, *tile), pltpu.VMEM((4, 128, 256), F32), buf(8, *tile), buf(8, *tile),
            pltpu.VMEM((1024, 128), F32), pltpu.VMEM((1024, 128), F32),
            buf(8, 2, *tile), buf(8, 2, *tile), buf(8, 2, *tile), buf(8, 2, *tile),
            buf(256, 512), buf(512, 256), buf(2, 256, 1024), buf(2, 256, 1024),
            pltpu.VMEM((2, 256, 1024), F32), buf(256, 1024), buf(256, 1024), buf(256, 1024),
            buf(4, 4, 32, 1024), buf(4, 4, 32, 1024),
            buf(4, 8, 32, 128), buf(4, 8, 32, 128), buf(4, 32, 128), buf(4, 32, 128),
            buf(512, 2048),
            dma((6,)), dma((11,)), dma, dma, dma((8,)), dma((8,)), dma((16,)), dma((16,)),
            dma((8,)), dma((8,)),
            dma((8,)), dma((8,)), dma((8,)), dma((8,)), dma, dma, dma((8,)), dma((8,)),
            dma((4,)), dma((4,)), dma, dma,
            dma((4, 3)), dma((4,)), dma((4,)), dma((4,)), dma((4,)), dma((4,)),
            dma((4,)), dma((4,)), dma((4,)), dma((4,)), dma((4,)), dma((4,)),
        ],
        compiler_params=pltpu.CompilerParams(
            collective_id=0, has_side_effects=True, vmem_limit_bytes=56 * 1024 * 1024),
        cost_estimate=pl.CostEstimate(
            flops=5 * 10**9, bytes_accessed=10 * 2**20, transcendentals=2 * 2**20),
        name="strip_attention",
    )(offs, queries.reshape(field), keys.reshape(field), values.reshape(field), w_out,
      grad_out.reshape(256, 1024))

    grid = jax.ShapeDtypeStruct(field, F32)
    layer, gq, gk, gv, gwo = pl.pallas_call(
        place_kernel,
        out_shape=(mid[0], grid, grid, grid, jax.ShapeDtypeStruct((512, 2048), F32)),
        in_specs=[any_spec] * 5,
        out_specs=(any_spec,) * 5,
        scratch_shapes=[
            pltpu.SMEM((2, 8), jnp.int32), buf(8, *tile), buf(8, 2, *tile), buf(512, 2048),
            buf(256, 1024), pltpu.VMEM((3,) + field, F32), pltpu.VMEM((512, 2048), F32),
            dma((8,)), dma((8,))],
        compiler_params=pltpu.CompilerParams(vmem_limit_bytes=60 * 1024 * 1024),
        cost_estimate=pl.CostEstimate(
            flops=10**8, bytes_accessed=10 * 2**20, transcendentals=0),
        name="place_gradients",
    )(offs, *parts)
    shape = queries.shape
    return (layer.reshape(grad_out.shape), gq.reshape(shape), gk.reshape(shape), gv.reshape(shape),
            gwo)


def solution(mesh):
    field = P("cam", "frame", None, None, "head")
    rows = P("cam", "frame", None, None, None, "head")
    return jax.shard_map(
        on_device,
        mesh=mesh,
        in_specs=(field, field, field, P(), P("head", None), rows),
        out_specs=(rows, field, field, field, P("head", None)),
        check_vma=False,
    )
```

time: 99.1 us -> 101 us (1.019)
  Pallas kernels: 98.3 us -> 99.8 us
    pallas_call x1, Pallas kernels: 93.6 us -> 95.2 us  [on_device(): pl.pallas_call(main_kernel, out_shape=mid, in_specs=[any_spec] * 6, out_s...]
where the time goes in v3:
time: 101 us; the launch traced here: 100 us
  Pallas kernels  99.8 us (99%)
    pallas_call x1, Pallas kernels, on_device(): pl.pallas_call(main_kernel, out_shape=mid, in_specs=[any_spec] * 6, out_s...  95.2 us
    pallas_call x1, Pallas kernels, on_device(): pl.pallas_call(place_kernel, out_shape=(mid[0], grid, grid, grid, jax.Sha...  4.54 us

profile of v3, /device:TPU:1, one launch (start us, length us, event | category | flops | bytes accessed | tf_op | source)
XLA Modules:
  0.0 100.4 jit_solution(4023831913577830223)
XLA Ops:
  0.6 95.2 %strip_attention.1 = (bf16[256,1024]{1,0:T(8,128)(2,1)}, bf16[8,128,128]{2,1,0:T(8,128)(2,1)}, bf16[8,2,128,128]{3,2,1,0:T(8,128)(2,1)}, bf16[512,2048]{1,0:T(8,128)(2,1)}) custom-call(s32[2,8]{1,0:T(2,128)} %bitcast.9, bf16[2,4,64,512]{3,2,1,0:T(8,128)(2,1)} %bitcast.14, bf16[2,4,64,512]{3,2,1,0:T(8,128)(2,1)} %bitcast.15, ...), custom_call_target="tpu_custom_call" | custom-call | flops 5000000000 | bytes 10485760 | tf_op jit(solution)/shard_map/strip_attention/pallas_call | solution.py:523
  95.9 4.5 %place_gradients.1 = (bf16[256,1024]{1,0:T(8,128)(2,1)}, f32[2,4,64,512]{3,2,1,0:T(8,128)}, f32[2,4,64,512]{3,2,1,0:T(8,128)}, f32[2,4,64,512]{3,2,1,0:T(8,128)}, f32[512,2048]{1,0:T(8,128)}) custom-call(s32[2,8]{1,0:T(2,128)} %bitcast.10, bf16[256,1024]{1,0:T(8,128)(2,1)} %get-tuple-element.14.lo_hbm, bf16[8,128,128]{2,1,0:T(8,128)(2,1)} %get-tuple-element.15.dq_hbm, ...), custom_call_target="tpu_custom_call" | custom-call | flops 100000000 | bytes 10485760 | tf_op jit(solution)/shard_map/place_gradients/pallas_call | solution.py:559

commit v4 on v3

--- a/solution.py
+++ b/solution.py
@@ -13,6 +13,7 @@
 MESH = pl.DeviceIdType.MESH
 LOG2E = 1.4426950408889634
 NT = (((1,), (1,)), ((), ()))
+PIECES = ("xz", "zx", "xz", "xz")
 
 
 def dot(a, b):
@@ -57,28 +58,31 @@
     kt, vt, probs, o_t, rl,
     att_send, att_recv, dq_acc, dq_send, dq_recv, dk_acc, dv_acc, far_send, far_recv, dkv_send, dkv_recv,
     a_rows, a_t, core_send, core_recv, own, lo_send, lo_recv, lo_done,
-    x_send, x_recv, z_send, z_recv, y_send, y_recv, gw,
+    out_bf, gw, first_recv, mid_sum, second_recv, y_send, y_recv,
     in_sem, out_sem, g_ss, g_rs, q_ss, q_rs, kv_ss, kv_rs, do_ss, do_rs,
     att_ss, att_rs, dq_ss, dq_rs, far_ss, far_rs, dkv_ss, dkv_rs, core_ss, core_rs, lo_ss, lo_rs,
-    x_ss, x_rs, z_ss, z_rs, y_ss, y_rs, zg_ss, zg_rs, xg_ss, xg_rs, cg_ss, cg_rs,
+    sum_ss, sum_rs,
 ):
     c = lax.axis_index("cam")
     f = lax.axis_index("frame")
     hh = lax.axis_index("head")
-    x, yh, k = f // 4, (f // 2) % 2, f % 2
+    x, yh, k = f >> 2, (f >> 1) & 1, f & 1
     u = x * 2 + k
     scale = HD ** (-0.5)
 
     def frame_of(unit):
-        return (unit // 2) * 4 + yh * 2 + unit % 2
+        return (unit >> 1) * 4 + yh * 2 + (unit & 1)
 
     def frame_x(to_x):
         return to_x * 4 + yh * 2 + k
+
+    def device(cam=c, frame=f, head=hh):
+        return (cam, frame, head)
 
     def remote(src, dst, ss, rs, **where):
         return pltpu.make_async_remote_copy(
             src_ref=src, dst_ref=dst, send_sem=ss, recv_sem=rs,
-            device_id=where, device_id_type=MESH)
+            device_id=device(**where), device_id_type=MESH)
 
     other_core = x * 4 + yh * 2 + 1 - k
     other_half = x * 4 + (1 - yh) * 2 + k
@@ -86,11 +90,11 @@
     barrier = pltpu.get_barrier_semaphore()
 
     def greet(**where):
-        pl.semaphore_signal(barrier, inc=1, device_id=where, device_id_type=MESH)
+        pl.semaphore_signal(barrier, inc=1, device_id=device(**where), device_id_type=MESH)
 
     def greet_cams(i):
-        greet(cam=(c + 1) % 8, frame=i)
-        greet(cam=(c + 7) % 8, frame=i)
+        greet(cam=(c + 1) & 7, frame=i)
+        greet(cam=(c + 7) & 7, frame=i)
 
     loads = [
         pltpu.make_async_copy(src, dst, in_sem.at[i])
@@ -101,8 +105,8 @@
     for load in loads:
         load.start()
     each(16, greet_cams)
-    each(7, lambda i: greet(frame=frame_of((u + 1 + i) % 8)))
-    each(5, lambda i: greet(cam=(c + 2 + i) % 8))
+    each(7, lambda i: greet(frame=frame_of((u + 1 + i) & 7)))
+    each(5, lambda i: greet(cam=(c + 2 + i) & 7))
     greet(frame=other_half)
     greet(head=1 - hh)
 
@@ -121,12 +125,15 @@
             for h in range(4):
                 kv_send[h * 2 + 1 - side, i] = cut[:, h * 128:(h + 1) * 128]
 
+    loads[3].wait()
     pl.semaphore_wait(barrier, 46)
+    g_copy = remote(gfull.at[hh], gfull.at[hh], g_ss, g_rs, head=1 - hh)
+    g_copy.start()
 
     def kv_copy(i):
-        unit, half = (u + i) % 8, (yh + 1 + i // 8) % 2
-        to_cam = (c + 9 - 2 * (unit % 2)) % 8
-        to_frame = (unit // 2) * 4 + half * 2 + unit % 2
+        unit, half = (u + i) & 7, (yh + 1 + (i >> 3)) & 1
+        to_cam = (c + 9 - 2 * (unit & 1)) & 7
+        to_frame = (unit >> 1) * 4 + half * 2 + (unit & 1)
         return remote(kv_send.at[unit], kv_recv.at[yh, u], kv_ss.at[i], kv_rs.at[yh * 8 + u],
                       cam=to_cam, frame=to_frame)
 
@@ -139,7 +146,7 @@
             q_send[h * 2 + side] = cut[:, h * 128:(h + 1) * 128]
 
     def half_copy(send, recv, ss, rs, i):
-        unit = (u + i) % 8
+        unit = (u + i) & 7
         return remote(send.at[unit], recv.at[u], ss.at[unit], rs.at[u], frame=frame_of(unit))
 
     def own_copy(send, recv, rs):
@@ -147,15 +154,12 @@
 
     own_copy(q_send, q_recv, q_rs).start()
     each(7, lambda i: half_copy(q_send, q_recv, q_ss, q_rs, i + 1).start())
-    loads[3].wait()
-    g_copy = remote(gfull.at[hh], gfull.at[hh], g_ss, g_rs, head=1 - hh)
-    g_copy.start()
 
     def arrived(ref, sem):
         pltpu.make_async_copy(ref, ref, sem).wait()
 
     def kv_arrive(i):
-        half, source = i // 8, i % 8
+        half, source = i >> 3, i & 7
         arrived(kv_recv.at[half, source], kv_rs.at[i])
         cols = pl.ds(pl.multiple_of(source * 128, 128), 128)
         vt[half, :, cols] = transposed(kv_recv[half, source, 1]).astype(BF)
@@ -176,7 +180,7 @@
                    frame=frame_of(unit)).start()
 
     def forward(i):
-        b = (x + i) % 4
+        b = (x + i) & 3
         for t in range(2):
             arrived(q_recv.at[2 * b + t], q_rs.at[2 * b + t])
         queries = q_recv[pl.ds(2 * b, 2)].reshape(256, 128)
@@ -200,6 +204,18 @@
 
     each(4, forward)
 
+    arrived(gfull.at[1 - hh], g_rs)
+    loads[4].wait()
+    grad_attn = dot_nt(gfull[0], w[:, :1024]) + dot_nt(gfull[1], w[:, 1024:])
+    grad_attn = grad_attn.astype(BF)
+    for fr in range(2):
+        for s in range(2):
+            for h in range(4):
+                do_send[h * 2 + s, fr * 64:(fr + 1) * 64] = grad_attn[
+                    fr * 128 + s * 64:fr * 128 + s * 64 + 64, h * 128:(h + 1) * 128]
+    own_copy(do_send, do_recv, do_rs).start()
+    each(7, lambda i: half_copy(do_send, do_recv, do_ss, do_rs, i + 1).start())
+
     each(8, lambda i: arrived(att_recv.at[i], att_rs.at[i]))
     for fr in range(2):
         for s in range(2):
@@ -211,107 +227,116 @@
             a_t[h * 128:(h + 1) * 128, fr * 128:(fr + 1) * 128] = transposed(
                 a_rows[fr * 128:(fr + 1) * 128, h * 128:(h + 1) * 128]).astype(BF)
 
-    features = (hh, 1 - hh)
-
     def core_copy(p):
-        part = (p // 2, pl.ds(p % 2 * 128, 128))
+        part = pl.ds(p * 64, 64)
         return remote(core_send.at[part], core_recv.at[part], core_ss.at[p], core_rs.at[p],
                       frame=other_core)
 
-    def multiply(g):
+    def multiply():
         theirs = a_t[pl.ds(pl.multiple_of((1 - k) * 256, 256), 256), :]
-        core_send[g] = dot(theirs, gfull[features[g]]).astype(BF)
-        core_copy(2 * g).start()
-        core_copy(2 * g + 1).start()
+        for j in range(2):
+            core_send[:, j * 1024:(j + 1) * 1024] = dot(theirs, gfull[j]).astype(BF)
+        for p in range(4):
+            core_copy(p).start()
         mine = a_t[pl.ds(pl.multiple_of(k * 256, 256), 256), :]
-        own[g] = dot(mine, gfull[features[g]])
-
-    def x_copy(p, i):
-        to = (x + i) % 4
-        return remote(x_send.at[p, to], x_recv.at[p, x], x_ss.at[p, i - 1], x_rs.at[p],
-                      frame=frame_x(to))
-
-    def core_total(p):
-        part = pl.ds(p % 2 * 128, 128)
-        arrived(core_recv.at[p // 2, part], core_rs.at[p])
-        piece = own[p // 2, part, :] + core_recv[p // 2, part, :].astype(F32)
-        own[p // 2, part, :] = piece
-        x_send[p] = piece.astype(BF).reshape(4, 32, 1024)
-        for i in (1, 3, 2):
-            x_copy(p, i).start()
-
-    def z_copy(p, i):
-        to = (c + i) % 8
-        return remote(z_send.at[p, to], z_recv.at[p, c], z_ss.at[p], z_rs.at[p], cam=to)
-
-    def x_total(p):
-        arrived(x_recv.at[p, pl.ds(0, 3)], x_rs.at[p])
-        total = own[p // 2, pl.ds(pl.multiple_of(p % 2 * 128 + x * 32, 32), 32), :]
-        for i in range(1, 4):
-            total = total + x_recv[p, (x + i) % 4].astype(F32)
-        total = total.astype(BF)
-        for i in range(8):
-            z_send[p, i] = total[:, i * 128:(i + 1) * 128]
-        each(7, lambda i: z_copy(p, i + 1).start())
+        for j in range(2):
+            own[:, j * 1024:(j + 1) * 1024] = dot(mine, gfull[j])
+
+    def peers(axis):
+        if axis == "x":
+            return [((x + i) & 3, dict(frame=frame_x((x + i) & 3))) for i in (1, 3, 2)]
+        return [((c + i) & 7, dict(cam=(c + i) & 7)) for i in (1, 7, 2, 6, 3, 5, 4)]
+
+    def area(p, axes, at_x=x, at_z=c, base=0):
+        rows, cols = pl.ds(base + p * 64, 64), pl.ds(0, 2048)
+        if "x" in axes:
+            rows = pl.ds(pl.multiple_of(base + p * 64 + at_x * 16, 16), 16)
+        elif not isinstance(base, int):
+            rows = pl.ds(pl.multiple_of(base + p * 64, 64), 64)
+        if "z" in axes:
+            cols = pl.ds(pl.multiple_of(at_z * 256, 256), 256)
+        return rows, cols
+
+    def me(axis):
+        return x if axis == "x" else c
+
+    def sum_copy(src, dst, p, step, where):
+        return remote(src, dst, sum_ss.at[p, step], sum_rs.at[p, step], **where)
+
+    def batch(recv, p, axis):
+        return recv[p].at[pl.ds(0, 3 if axis == "x" else 7)]
+
+    def first_sent(p):
+        arrived(batch(first_recv, p, PIECES[p][0]), sum_ss.at[p, 0])
+
+    def first(p):
+        part = pl.ds(p * 64, 64)
+        axis = PIECES[p][0]
+        arrived(core_recv.at[part], core_rs.at[p])
+        own[part, :] += core_recv[part, :].astype(F32)
+        out_bf[part, :] = own[part, :].astype(BF)
+        for to, where in peers(axis):
+            src = out_bf.at[area(p, axis, to, to)]
+            sum_copy(src, first_recv[p].at[me(axis)], p, 0, where).start()
+
+    def second(p):
+        axis, other = PIECES[p]
+        arrived(batch(first_recv, p, axis), sum_rs.at[p, 0])
+        total = own[area(p, axis)]
+        for frm, _ in peers(axis):
+            total = total + first_recv[p][frm].astype(F32)
+        mid_sum[p][...] = total.astype(BF)
+        for to, where in peers(other):
+            sum_copy(mid_sum[p].at[mid_part(p, to)], second_recv[p].at[me(other)], p, 1, where).start()
+
+    def mid_part(p, to):
+        if PIECES[p][1] == "x":
+            return pl.ds(pl.multiple_of(to * 16, 16), 16), pl.ds(0, 256)
+        return pl.ds(0, 16), pl.ds(pl.multiple_of(to * 256, 256), 256)
 
     def y_copy(p):
-        return remote(y_send.at[p], y_recv.at[p], y_ss.at[p], y_rs.at[p], frame=other_half)
-
-    def z_total(p):
-        arrived(z_recv.at[p, pl.ds(0, 7)], z_rs.at[p])
-        total = z_send[p, c].astype(F32)
-        for i in range(1, 8):
-            total = total + z_recv[p, (c + i) % 8].astype(F32)
+        return sum_copy(y_send.at[p], y_recv.at[p], p, 2, dict(frame=other_half))
+
+    def third(p):
+        axis = PIECES[p][1]
+        arrived(batch(second_recv, p, axis), sum_rs.at[p, 1])
+        total = mid_sum[p][mid_part(p, me(axis))].astype(F32)
+        for frm, _ in peers(axis):
+            total = total + second_recv[p][frm].astype(F32)
         y_send[p] = total.astype(BF)
         y_copy(p).start()
 
-    def piece_at(p, core, to_x=None, z=None):
-        row, rows = core * 256 + p % 2 * 128, 128
-        if to_x is not None:
-            row, rows = row + to_x * 32, 32
-        col, cols = features[p // 2] * 1024, 1024
-        if z is not None:
-            col, cols = col + z * 128, 128
-        return (pl.ds(pl.multiple_of(row, rows), rows), pl.ds(pl.multiple_of(col, cols), cols))
-
-    def zg_copy(p, i):
-        part = gw.at[piece_at(p, k, x, c)]
-        return remote(part, part, zg_ss.at[p], zg_rs.at[p], cam=(c + i) % 8)
-
-    def y_total(p):
-        arrived(y_recv.at[p], y_rs.at[p])
-        rows, cols = piece_at(p, k, x, c)
-        gw[rows, cols] = (y_send[p].astype(F32) + y_recv[p].astype(F32)).astype(BF)
-        each(7, lambda i: zg_copy(p, i + 1).start())
-
-    def xg_copy(p, i):
-        part = gw.at[piece_at(p, k, x)]
-        return remote(part, part, xg_ss.at[p], xg_rs.at[p], frame=frame_x((x + i) % 4))
-
-    def z_gathered(p):
-        arrived(z_recv.at[p, pl.ds(0, 7)], zg_rs.at[p])
-        for i in (1, 3, 2):
-            xg_copy(p, i).start()
-
-    def cg_copy(p):
-        part = gw.at[piece_at(p, k)]
-        return remote(part, part, cg_ss.at[p], cg_rs.at[p], frame=other_core)
+    def gather(p, axes, axis, step):
+        part = gw.at[area(p, axes, base=k * 256)]
+        for _, where in peers(axis):
+            sum_copy(part, part, p, step, where).start()
+
+    def fourth(p):
+        arrived(y_recv.at[p], sum_rs.at[p, 2])
+        gw[area(p, "xz", base=k * 256)] = (
+            y_send[p].astype(F32) + y_recv[p].astype(F32)).astype(BF)
+        gather(p, "xz", PIECES[p][1], 3)
+
+    def fifth(p):
+        arrived(batch(second_recv, p, PIECES[p][1]), sum_rs.at[p, 3])
+        gather(p, PIECES[p][0], PIECES[p][0], 4)
+
+    def sixth(p):
+        arrived(batch(first_recv, p, PIECES[p][0]), sum_rs.at[p, 4])
+        part = gw.at[area(p, "", base=k * 256)]
+        sum_copy(part, part, p, 5, dict(frame=other_core)).start()
+        gw_write(p, k).start()
+
+    def seventh(p):
+        arrived(gw.at[area(p, "", base=(1 - k) * 256)], sum_rs.at[p, 5])
+        gw_write(p, 1 - k).start()
 
     def gw_write(p, core):
-        at = piece_at(p, core)
+        at = area(p, "", base=core * 256)
         return pltpu.make_async_copy(gw.at[at], gw_hbm.at[at], out_sem.at[3 + p * 2 + core])
 
-    def x_gathered(p):
-        arrived(x_recv.at[p, pl.ds(0, 3)], xg_rs.at[p])
-        cg_copy(p).start()
-        gw_write(p, k).start()
-
-    def core_gathered(p):
-        arrived(gw.at[piece_at(p, 1 - k)], cg_rs.at[p])
-        gw_write(p, 1 - k).start()
-
     def backward(half, i):
-        b = (x + i) % 4
+        b = (x + i) & 3
         if half is far:
             for t in range(2):
                 arrived(do_recv.at[2 * b + t], do_rs.at[2 * b + t])
@@ -341,67 +366,54 @@
         return remote(far_send, far_recv, far_ss, far_rs, frame=other_half)
 
     def dkv_copy(i):
-        source = (u + i) % 8
+        source = (u + i) & 7
         return remote(dkv_send.at[source], dkv_recv.at[u], dkv_ss.at[i], dkv_rs.at[u],
-                      cam=(c + 7 + 2 * k) % 8, frame=frame_of(source))
+                      cam=(c + 7 + 2 * k) & 7, frame=frame_of(source))
 
     far, near = 1 - yh, yh
 
-    multiply(0)
-
     def key_turn(i):
-        half, source = i // 8, i % 8
+        half, source = i >> 3, i & 7
         kt[half, :, pl.ds(pl.multiple_of(source * 128, 128), 128)] = transposed(
             kv_recv[half, source, 0]).astype(BF)
 
-    core_total(0)
-    core_total(1)
-    each(16, key_turn)
-    arrived(gfull.at[1 - hh], g_rs)
-    loads[4].wait()
-    grad_attn = dot_nt(gfull[0], w[:, :1024]) + dot_nt(gfull[1], w[:, 1024:])
-    grad_attn = grad_attn.astype(BF)
-    for fr in range(2):
-        for s in range(2):
-            for h in range(4):
-                do_send[h * 2 + s, fr * 64:(fr + 1) * 64] = grad_attn[
-                    fr * 128 + s * 64:fr * 128 + s * 64 + 64, h * 128:(h + 1) * 128]
-    own_copy(do_send, do_recv, do_rs).start()
-    each(7, lambda i: half_copy(do_send, do_recv, do_ss, do_rs, i + 1).start())
-    multiply(1)
-    x_total(0)
-    x_total(1)
+    multiply()
+    first(0)
+    first(1)
     lo_send[...] = dot(
         a_rows[...], w[:, pl.ds(pl.multiple_of((1 - hh) * 1024, 1024), 1024)]).astype(BF)
     lo_copy = remote(lo_send, lo_recv, lo_ss, lo_rs, head=1 - hh)
     lo_copy.start()
-    core_total(2)
-    core_total(3)
+    each(16, key_turn)
+    first_sent(0)
+    first(2)
     backward(far, 0)
+    second(0)
     backward(far, 1)
-    z_total(0)
-    z_total(1)
+    first_sent(2)
+    first(3)
     backward(far, 2)
+    second(1)
     backward(far, 3)
     far_send[:, 0] = dk_acc[...].astype(BF).reshape(8, 128, 128)
     far_send[:, 1] = dv_acc[...].astype(BF).reshape(8, 128, 128)
     far_copy().start()
-    x_total(2)
-    x_total(3)
-    y_total(0)
-    y_total(1)
+    second(2)
+    third(0)
     backward(near, 0)
+    second(3)
+    third(1)
     backward(near, 1)
-    z_total(2)
-    z_total(3)
-    z_gathered(0)
-    z_gathered(1)
+    third(2)
+    fourth(0)
     backward(near, 2)
+    third(3)
+    fourth(1)
+    fourth(2)
     backward(near, 3)
-    y_total(2)
-    y_total(3)
-    x_gathered(0)
-    x_gathered(1)
+    fourth(3)
+    fifth(0)
+    fifth(1)
     far_copy().wait()
     for i, acc in enumerate((dk_acc, dv_acc)):
         total = acc[...].reshape(8, 128, 128) + far_recv[:, i].astype(F32)
@@ -409,27 +421,28 @@
             total = total * scale
         dkv_send[:, i] = total.astype(BF)
     each(8, lambda i: dkv_copy(i).start())
-    z_gathered(2)
-    z_gathered(3)
+    fifth(2)
+    fifth(3)
 
     here = dot(a_rows[...], w[:, pl.ds(pl.multiple_of(hh * 1024, 1024), 1024)])
     lo_copy.wait()
     lo_done[...] = (here + lo_recv[...].astype(F32)).astype(BF)
     lo_write = pltpu.make_async_copy(lo_done, lo_hbm, out_sem.at[0])
     lo_write.start()
-
-    core_gathered(0)
-    core_gathered(1)
+    sixth(0)
+    sixth(1)
     each(8, lambda i: arrived(dq_recv.at[i], dq_rs.at[i]))
     dq_write = pltpu.make_async_copy(dq_recv, dq_hbm, out_sem.at[1])
     dq_write.start()
+    sixth(2)
+    seventh(0)
+    seventh(1)
+    sixth(3)
     each(8, lambda i: arrived(dkv_recv.at[i], dkv_rs.at[i]))
     dkv_write = pltpu.make_async_copy(dkv_recv, dkv_hbm, out_sem.at[2])
     dkv_write.start()
-    x_gathered(2)
-    x_gathered(3)
-    core_gathered(2)
-    core_gathered(3)
+    seventh(2)
+    seventh(3)
 
     g_copy.wait_send()
     each(16, lambda i: kv_copy(i).wait_send())
@@ -442,15 +455,16 @@
     sent(att_send, att_recv, att_ss, att_rs)
     sent(dq_send, dq_recv, dq_ss, dq_rs)
     each(8, lambda i: dkv_copy(i).wait_send())
+    first_sent(1)
+    first_sent(3)
     for p in range(4):
+        axis, other = PIECES[p]
         core_copy(p).wait_send()
-        for i in (1, 2, 3):
-            x_copy(p, i).wait_send()
-        arrived(z_recv.at[p, pl.ds(0, 7)], z_ss.at[p])
+        arrived(batch(second_recv, p, other), sum_ss.at[p, 1])
         y_copy(p).wait_send()
-        arrived(z_recv.at[p, pl.ds(0, 7)], zg_ss.at[p])
-        arrived(x_recv.at[p, pl.ds(0, 3)], xg_ss.at[p])
-        cg_copy(p).wait_send()
+        arrived(batch(second_recv, p, other), sum_ss.at[p, 3])
+        arrived(batch(first_recv, p, axis), sum_ss.at[p, 4])
+        arrived(gw.at[area(p, "", base=k * 256)], sum_ss.at[p, 5])
         gw_write(p, k).wait()
         gw_write(p, 1 - k).wait()
     lo_write.wait()
@@ -535,17 +549,18 @@
             buf(8, *tile), buf(8, *tile), pltpu.VMEM((4, 128, 256), F32), buf(8, *tile), buf(8, *tile),
             pltpu.VMEM((1024, 128), F32), pltpu.VMEM((1024, 128), F32),
             buf(8, 2, *tile), buf(8, 2, *tile), buf(8, 2, *tile), buf(8, 2, *tile),
-            buf(256, 512), buf(512, 256), buf(2, 256, 1024), buf(2, 256, 1024),
-            pltpu.VMEM((2, 256, 1024), F32), buf(256, 1024), buf(256, 1024), buf(256, 1024),
-            buf(4, 4, 32, 1024), buf(4, 4, 32, 1024),
-            buf(4, 8, 32, 128), buf(4, 8, 32, 128), buf(4, 32, 128), buf(4, 32, 128),
-            buf(512, 2048),
+            buf(256, 512), buf(512, 256), buf(256, 2048), buf(256, 2048),
+            pltpu.VMEM((256, 2048), F32), buf(256, 1024), buf(256, 1024), buf(256, 1024),
+            buf(256, 2048), buf(512, 2048),
+            [buf(4, 16, 2048) if axes == "xz" else buf(8, 64, 256) for axes in PIECES],
+            [buf(16, 2048) if axes == "xz" else buf(64, 256) for axes in PIECES],
+            [buf(8, 16, 256) if axes == "xz" else buf(4, 16, 256) for axes in PIECES],
+            buf(4, 16, 256), buf(4, 16, 256),
             dma((6,)), dma((11,)), dma, dma, dma((8,)), dma((8,)), dma((16,)), dma((16,)),
             dma((8,)), dma((8,)),
             dma((8,)), dma((8,)), dma((8,)), dma((8,)), dma, dma, dma((8,)), dma((8,)),
             dma((4,)), dma((4,)), dma, dma,
-            dma((4, 3)), dma((4,)), dma((4,)), dma((4,)), dma((4,)), dma((4,)),
-            dma((4,)), dma((4,)), dma((4,)), dma((4,)), dma((4,)), dma((4,)),
+            dma((4, 6)), dma((4, 6)),
         ],
         compiler_params=pltpu.CompilerParams(
             collective_id=0, has_side_effects=True, vmem_limit_bytes=56 * 1024 * 1024),

time: 101 us -> 99.2 us (0.982)
  Pallas kernels: 99.8 us -> 98.4 us
    pallas_call x1, Pallas kernels: 95.2 us -> 93.9 us  [on_device(): pl.pallas_call(main_kernel, out_shape=mid, in_specs=[any_spec] * 6, out_s...]
where the time goes in v4:
time: 99.2 us; the launch traced here: 99.1 us
  Pallas kernels  98.4 us (99%)
    pallas_call x1, Pallas kernels, on_device(): pl.pallas_call(main_kernel, out_shape=mid, in_specs=[any_spec] * 6, out_s...  93.9 us
    pallas_call x1, Pallas kernels, on_device(): pl.pallas_call(place_kernel, out_shape=(mid[0], grid, grid, grid, jax.Sha...  4.54 us

profile of v4, /device:TPU:1, one launch (start us, length us, event | category | flops | bytes accessed | tf_op | source)
XLA Modules:
  0.0 99.1 jit_solution(4433721363504353837)
XLA Ops:
  0.6 93.9 %strip_attention.1 = (bf16[256,1024]{1,0:T(8,128)(2,1)}, bf16[8,128,128]{2,1,0:T(8,128)(2,1)}, bf16[8,2,128,128]{3,2,1,0:T(8,128)(2,1)}, bf16[512,2048]{1,0:T(8,128)(2,1)}) custom-call(s32[2,8]{1,0:T(2,128)} %bitcast.9, bf16[2,4,64,512]{3,2,1,0:T(8,128)(2,1)} %bitcast.14, bf16[2,4,64,512]{3,2,1,0:T(8,128)(2,1)} %bitcast.15, ...), custom_call_target="tpu_custom_call" | custom-call | flops 5000000000 | bytes 10485760 | tf_op jit(solution)/shard_map/strip_attention/pallas_call | solution.py:537
  94.5 4.5 %place_gradients.1 = (bf16[256,1024]{1,0:T(8,128)(2,1)}, f32[2,4,64,512]{3,2,1,0:T(8,128)}, f32[2,4,64,512]{3,2,1,0:T(8,128)}, f32[2,4,64,512]{3,2,1,0:T(8,128)}, f32[512,2048]{1,0:T(8,128)}) custom-call(s32[2,8]{1,0:T(2,128)} %bitcast.10, bf16[256,1024]{1,0:T(8,128)(2,1)} %get-tuple-element.14.lo_hbm, bf16[8,128,128]{2,1,0:T(8,128)(2,1)} %get-tuple-element.15.dq_hbm, ...), custom_call_target="tpu_custom_call" | custom-call | flops 100000000 | bytes 10485760 | tf_op jit(solution)/shard_map/place_gradients/pallas_call | solution.py:574

commit v5 on v4

--- a/solution.py
+++ b/solution.py
@@ -125,10 +125,7 @@
             for h in range(4):
                 kv_send[h * 2 + 1 - side, i] = cut[:, h * 128:(h + 1) * 128]
 
-    loads[3].wait()
     pl.semaphore_wait(barrier, 46)
-    g_copy = remote(gfull.at[hh], gfull.at[hh], g_ss, g_rs, head=1 - hh)
-    g_copy.start()
 
     def kv_copy(i):
         unit, half = (u + i) & 7, (yh + 1 + (i >> 3)) & 1
@@ -154,6 +151,9 @@
 
     own_copy(q_send, q_recv, q_rs).start()
     each(7, lambda i: half_copy(q_send, q_recv, q_ss, q_rs, i + 1).start())
+    loads[3].wait()
+    g_copy = remote(gfull.at[hh], gfull.at[hh], g_ss, g_rs, head=1 - hh)
+    g_copy.start()
 
     def arrived(ref, sem):
         pltpu.make_async_copy(ref, ref, sem).wait()
@@ -215,6 +215,13 @@
                     fr * 128 + s * 64:fr * 128 + s * 64 + 64, h * 128:(h + 1) * 128]
     own_copy(do_send, do_recv, do_rs).start()
     each(7, lambda i: half_copy(do_send, do_recv, do_ss, do_rs, i + 1).start())
+
+    def key_turn(i):
+        half, source = i >> 3, i & 7
+        kt[half, :, pl.ds(pl.multiple_of(source * 128, 128), 128)] = transposed(
+            kv_recv[half, source, 0]).astype(BF)
+
+    each(16, key_turn)
 
     each(8, lambda i: arrived(att_recv.at[i], att_rs.at[i]))
     for fr in range(2):
@@ -372,46 +379,38 @@
 
     far, near = 1 - yh, yh
 
-    def key_turn(i):
-        half, source = i >> 3, i & 7
-        kt[half, :, pl.ds(pl.multiple_of(source * 128, 128), 128)] = transposed(
-            kv_recv[half, source, 0]).astype(BF)
-
     multiply()
+    for i in range(4):
+        backward(far, i)
+    far_send[:, 0] = dk_acc[...].astype(BF).reshape(8, 128, 128)
+    far_send[:, 1] = dv_acc[...].astype(BF).reshape(8, 128, 128)
+    far_copy().start()
     first(0)
     first(1)
+    backward(near, 0)
+    first_sent(0)
+    first(2)
+    backward(near, 1)
+    second(0)
+    first_sent(2)
+    first(3)
+    backward(near, 2)
+    second(1)
+    backward(near, 3)
+    second(2)
+    third(0)
+    second(3)
+    third(1)
+    third(2)
+    fourth(0)
+    third(3)
+    fourth(1)
+    fourth(2)
+    fourth(3)
     lo_send[...] = dot(
         a_rows[...], w[:, pl.ds(pl.multiple_of((1 - hh) * 1024, 1024), 1024)]).astype(BF)
     lo_copy = remote(lo_send, lo_recv, lo_ss, lo_rs, head=1 - hh)
     lo_copy.start()
-    each(16, key_turn)
-    first_sent(0)
-    first(2)
-    backward(far, 0)
-    second(0)
-    backward(far, 1)
-    first_sent(2)
-    first(3)
-    backward(far, 2)
-    second(1)
-    backward(far, 3)
-    far_send[:, 0] = dk_acc[...].astype(BF).reshape(8, 128, 128)
-    far_send[:, 1] = dv_acc[...].astype(BF).reshape(8, 128, 128)
-    far_copy().start()
-    second(2)
-    third(0)
-    backward(near, 0)
-    second(3)
-    third(1)
-    backward(near, 1)
-    third(2)
-    fourth(0)
-    backward(near, 2)
-    third(3)
-    fourth(1)
-    fourth(2)
-    backward(near, 3)
-    fourth(3)
     fifth(0)
     fifth(1)
     far_copy().wait()
@@ -424,25 +423,24 @@
     fifth(2)
     fifth(3)
 
-    here = dot(a_rows[...], w[:, pl.ds(pl.multiple_of(hh * 1024, 1024), 1024)])
-    lo_copy.wait()
-    lo_done[...] = (here + lo_recv[...].astype(F32)).astype(BF)
-    lo_write = pltpu.make_async_copy(lo_done, lo_hbm, out_sem.at[0])
-    lo_write.start()
-    sixth(0)
-    sixth(1)
+    lo_done[...] = dot(
+        a_rows[...], w[:, pl.ds(pl.multiple_of(hh * 1024, 1024), 1024)])
     each(8, lambda i: arrived(dq_recv.at[i], dq_rs.at[i]))
     dq_write = pltpu.make_async_copy(dq_recv, dq_hbm, out_sem.at[1])
     dq_write.start()
+    sixth(0)
+    sixth(1)
     sixth(2)
-    seventh(0)
-    seventh(1)
     sixth(3)
     each(8, lambda i: arrived(dkv_recv.at[i], dkv_rs.at[i]))
     dkv_write = pltpu.make_async_copy(dkv_recv, dkv_hbm, out_sem.at[2])
     dkv_write.start()
-    seventh(2)
-    seventh(3)
+    lo_copy.wait()
+    lo_send[...] = (lo_done[...] + lo_recv[...].astype(F32)).astype(BF)
+    lo_write = pltpu.make_async_copy(lo_send, lo_hbm, out_sem.at[0])
+    lo_write.start()
+    for p in range(4):
+        seventh(p)
 
     g_copy.wait_send()
     each(16, lambda i: kv_copy(i).wait_send())
@@ -550,7 +548,7 @@
             pltpu.VMEM((1024, 128), F32), pltpu.VMEM((1024, 128), F32),
             buf(8, 2, *tile), buf(8, 2, *tile), buf(8, 2, *tile), buf(8, 2, *tile),
             buf(256, 512), buf(512, 256), buf(256, 2048), buf(256, 2048),
-            pltpu.VMEM((256, 2048), F32), buf(256, 1024), buf(256, 1024), buf(256, 1024),
+            pltpu.VMEM((256, 2048), F32), buf(256, 1024), buf(256, 1024), pltpu.VMEM((256, 1024), F32),
             buf(256, 2048), buf(512, 2048),
             [buf(4, 16, 2048) if axes == "xz" else buf(8, 64, 256) for axes in PIECES],
             [buf(16, 2048) if axes == "xz" else buf(64, 256) for axes in PIECES],

time: 99.2 us -> 93.3 us (0.941)
  Pallas kernels: 98.4 us -> 92.4 us
    pallas_call x1, Pallas kernels: 93.9 us -> 87.8 us  [on_device(): pl.pallas_call(main_kernel, out_shape=mid, in_specs=[any_spec] * 6, out_s...]
where the time goes in v5:
time: 93.3 us; the launch traced here: 93.2 us
  Pallas kernels  92.4 us (99%)
    pallas_call x1, Pallas kernels, on_device(): pl.pallas_call(main_kernel, out_shape=mid, in_specs=[any_spec] * 6, out_s...  87.8 us
    pallas_call x1, Pallas kernels, on_device(): pl.pallas_call(place_kernel, out_shape=(mid[0], grid, grid, grid, jax.Sha...  4.53 us

profile of v5, /device:TPU:1, one launch (start us, length us, event | category | flops | bytes accessed | tf_op | source)
XLA Modules:
  0.0 93.2 jit_solution(13940747904653243278)
XLA Ops:
  0.6 87.8 %strip_attention.1 = (bf16[256,1024]{1,0:T(8,128)(2,1)}, bf16[8,128,128]{2,1,0:T(8,128)(2,1)}, bf16[8,2,128,128]{3,2,1,0:T(8,128)(2,1)}, bf16[512,2048]{1,0:T(8,128)(2,1)}) custom-call(s32[2,8]{1,0:T(2,128)} %bitcast.9, bf16[2,4,64,512]{3,2,1,0:T(8,128)(2,1)} %bitcast.14, bf16[2,4,64,512]{3,2,1,0:T(8,128)(2,1)} %bitcast.15, ...), custom_call_target="tpu_custom_call" | custom-call | flops 5000000000 | bytes 10485760 | tf_op jit(solution)/shard_map/strip_attention/pallas_call | solution.py:535
  88.5 4.5 %place_gradients.1 = (bf16[256,1024]{1,0:T(8,128)(2,1)}, f32[2,4,64,512]{3,2,1,0:T(8,128)}, f32[2,4,64,512]{3,2,1,0:T(8,128)}, f32[2,4,64,512]{3,2,1,0:T(8,128)}, f32[512,2048]{1,0:T(8,128)}) custom-call(s32[2,8]{1,0:T(2,128)} %bitcast.10, bf16[256,1024]{1,0:T(8,128)(2,1)} %get-tuple-element.14.lo_hbm, bf16[8,128,128]{2,1,0:T(8,128)(2,1)} %get-tuple-element.15.dq_hbm, ...), custom_call_target="tpu_custom_call" | custom-call | flops 100000000 | bytes 10485760 | tf_op jit(solution)/shard_map/place_gradients/pallas_call | solution.py:572

commit v6 on v5

--- a/solution.py
+++ b/solution.py
@@ -59,7 +59,7 @@
     att_send, att_recv, dq_acc, dq_send, dq_recv, dk_acc, dv_acc, far_send, far_recv, dkv_send, dkv_recv,
     a_rows, a_t, core_send, core_recv, own, lo_send, lo_recv, lo_done,
     out_bf, gw, first_recv, mid_sum, second_recv, y_send, y_recv,
-    in_sem, out_sem, g_ss, g_rs, q_ss, q_rs, kv_ss, kv_rs, do_ss, do_rs,
+    in_sem, out_sem, g_ss, g_rs, q_ss, q_rs, kv_ss, kv_rs, hand_ss, hand_rs, do_ss, do_rs,
     att_ss, att_rs, dq_ss, dq_rs, far_ss, far_rs, dkv_ss, dkv_rs, core_ss, core_rs, lo_ss, lo_rs,
     sum_ss, sum_rs,
 ):
@@ -67,11 +67,11 @@
     f = lax.axis_index("frame")
     hh = lax.axis_index("head")
     x, yh, k = f >> 2, (f >> 1) & 1, f & 1
-    u = x * 2 + k
+    u = x * 2 + yh
     scale = HD ** (-0.5)
 
     def frame_of(unit):
-        return (unit >> 1) * 4 + yh * 2 + (unit & 1)
+        return unit * 2 + k
 
     def frame_x(to_x):
         return to_x * 4 + yh * 2 + k
@@ -93,8 +93,8 @@
         pl.semaphore_signal(barrier, inc=1, device_id=device(**where), device_id_type=MESH)
 
     def greet_cams(i):
-        greet(cam=(c + 1) & 7, frame=i)
-        greet(cam=(c + 7) & 7, frame=i)
+        greet(cam=(c + 1) & 7, frame=frame_of(i))
+        greet(cam=(c + 7) & 7, frame=frame_of(i))
 
     loads = [
         pltpu.make_async_copy(src, dst, in_sem.at[i])
@@ -104,10 +104,10 @@
     ]
     for load in loads:
         load.start()
-    each(16, greet_cams)
+    each(8, greet_cams)
     each(7, lambda i: greet(frame=frame_of((u + 1 + i) & 7)))
     each(5, lambda i: greet(cam=(c + 2 + i) & 7))
-    greet(frame=other_half)
+    greet(frame=other_core)
     greet(head=1 - hh)
 
     loads[5].wait()
@@ -125,16 +125,14 @@
             for h in range(4):
                 kv_send[h * 2 + 1 - side, i] = cut[:, h * 128:(h + 1) * 128]
 
-    pl.semaphore_wait(barrier, 46)
+    pl.semaphore_wait(barrier, 30)
 
     def kv_copy(i):
-        unit, half = (u + i) & 7, (yh + 1 + (i >> 3)) & 1
-        to_cam = (c + 9 - 2 * (unit & 1)) & 7
-        to_frame = (unit >> 1) * 4 + half * 2 + (unit & 1)
-        return remote(kv_send.at[unit], kv_recv.at[yh, u], kv_ss.at[i], kv_rs.at[yh * 8 + u],
-                      cam=to_cam, frame=to_frame)
-
-    each(16, lambda i: kv_copy(i).start())
+        unit = (u + i) & 7
+        return remote(kv_send.at[unit], kv_recv.at[k, u], kv_ss.at[i], kv_rs.at[u],
+                      cam=(c + 9 - 2 * (unit & 1)) & 7, frame=frame_of(unit))
+
+    each(8, lambda i: kv_copy(i).start())
 
     loads[2].wait()
     for side in range(2):
@@ -158,13 +156,27 @@
     def arrived(ref, sem):
         pltpu.make_async_copy(ref, ref, sem).wait()
 
+    def turn(turned, half, source, i):
+        cols = pl.ds(pl.multiple_of(source * 128, 128), 128)
+        turned[half, :, cols] = transposed(kv_recv[half, source, i]).astype(BF)
+
+    def hand_copy(source):
+        part = kv_recv.at[k, source]
+        return remote(part, part, hand_ss.at[source], hand_rs.at[source], frame=other_core)
+
     def kv_arrive(i):
-        half, source = i >> 3, i & 7
-        arrived(kv_recv.at[half, source], kv_rs.at[i])
-        cols = pl.ds(pl.multiple_of(source * 128, 128), 128)
-        vt[half, :, cols] = transposed(kv_recv[half, source, 1]).astype(BF)
-
-    each(16, kv_arrive)
+        source = (u + 8 - i) & 7
+        arrived(kv_recv.at[k, source], kv_rs.at[source])
+        hand_copy(source).start()
+        turn(vt, k, source, 1)
+
+    def kv_handed(i):
+        source = (u + 8 - i) & 7
+        arrived(kv_recv.at[1 - k, source], hand_rs.at[source])
+        turn(vt, 1 - k, source, 1)
+
+    each(8, kv_arrive)
+    each(8, kv_handed)
 
     def stacked(half, i):
         return kv_recv[half, :, i].reshape(1024, 128)
@@ -216,12 +228,7 @@
     own_copy(do_send, do_recv, do_rs).start()
     each(7, lambda i: half_copy(do_send, do_recv, do_ss, do_rs, i + 1).start())
 
-    def key_turn(i):
-        half, source = i >> 3, i & 7
-        kt[half, :, pl.ds(pl.multiple_of(source * 128, 128), 128)] = transposed(
-            kv_recv[half, source, 0]).astype(BF)
-
-    each(16, key_turn)
+    each(16, lambda i: turn(kt, i >> 3, i & 7, 0))
 
     each(8, lambda i: arrived(att_recv.at[i], att_rs.at[i]))
     for fr in range(2):
@@ -370,33 +377,40 @@
             dv_acc[...] += dot(weights, grads)
 
     def far_copy():
-        return remote(far_send, far_recv, far_ss, far_rs, frame=other_half)
+        return remote(far_send, far_recv, far_ss, far_rs, frame=other_core)
 
     def dkv_copy(i):
         source = (u + i) & 7
         return remote(dkv_send.at[source], dkv_recv.at[u], dkv_ss.at[i], dkv_rs.at[u],
-                      cam=(c + 7 + 2 * k) & 7, frame=frame_of(source))
-
-    far, near = 1 - yh, yh
+                      cam=(c + 7 + 2 * yh) & 7, frame=frame_of(source))
+
+    far, near = 1 - k, k
 
     multiply()
+    first(0)
+    first(1)
     for i in range(4):
         backward(far, i)
     far_send[:, 0] = dk_acc[...].astype(BF).reshape(8, 128, 128)
     far_send[:, 1] = dv_acc[...].astype(BF).reshape(8, 128, 128)
     far_copy().start()
-    first(0)
-    first(1)
-    backward(near, 0)
     first_sent(0)
     first(2)
+    backward(near, 0)
+    second(0)
     backward(near, 1)
-    second(0)
     first_sent(2)
     first(3)
     backward(near, 2)
     second(1)
     backward(near, 3)
+    far_copy().wait()
+    for i, acc in enumerate((dk_acc, dv_acc)):
+        total = acc[...].reshape(8, 128, 128) + far_recv[:, i].astype(F32)
+        if i == 0:
+            total = total * scale
+        dkv_send[:, i] = total.astype(BF)
+    each(8, lambda i: dkv_copy(i).start())
     second(2)
     third(0)
     second(3)
@@ -413,13 +427,6 @@
     lo_copy.start()
     fifth(0)
     fifth(1)
-    far_copy().wait()
-    for i, acc in enumerate((dk_acc, dv_acc)):
-        total = acc[...].reshape(8, 128, 128) + far_recv[:, i].astype(F32)
-        if i == 0:
-            total = total * scale
-        dkv_send[:, i] = total.astype(BF)
-    each(8, lambda i: dkv_copy(i).start())
     fifth(2)
     fifth(3)
 
@@ -428,22 +435,12 @@
     each(8, lambda i: arrived(dq_recv.at[i], dq_rs.at[i]))
     dq_write = pltpu.make_async_copy(dq_recv, dq_hbm, out_sem.at[1])
     dq_write.start()
-    sixth(0)
-    sixth(1)
-    sixth(2)
-    sixth(3)
     each(8, lambda i: arrived(dkv_recv.at[i], dkv_rs.at[i]))
     dkv_write = pltpu.make_async_copy(dkv_recv, dkv_hbm, out_sem.at[2])
     dkv_write.start()
-    lo_copy.wait()
-    lo_send[...] = (lo_done[...] + lo_recv[...].astype(F32)).astype(BF)
-    lo_write = pltpu.make_async_copy(lo_send, lo_hbm, out_sem.at[0])
-    lo_write.start()
-    for p in range(4):
-        seventh(p)
-
     g_copy.wait_send()
-    each(16, lambda i: kv_copy(i).wait_send())
+    each(8, lambda i: kv_copy(i).wait_send())
+    each(8, lambda i: hand_copy(i).wait_send())
 
     def sent(send, recv, ss, rs):
         each(7, lambda i: half_copy(send, recv, ss, rs, i + 1).wait_send())
@@ -456,12 +453,23 @@
     first_sent(1)
     first_sent(3)
     for p in range(4):
-        axis, other = PIECES[p]
         core_copy(p).wait_send()
-        arrived(batch(second_recv, p, other), sum_ss.at[p, 1])
+        arrived(batch(second_recv, p, PIECES[p][1]), sum_ss.at[p, 1])
         y_copy(p).wait_send()
-        arrived(batch(second_recv, p, other), sum_ss.at[p, 3])
-        arrived(batch(first_recv, p, axis), sum_ss.at[p, 4])
+        arrived(batch(second_recv, p, PIECES[p][1]), sum_ss.at[p, 3])
+    sixth(0)
+    sixth(1)
+    sixth(2)
+    sixth(3)
+    lo_copy.wait()
+    lo_send[...] = (lo_done[...] + lo_recv[...].astype(F32)).astype(BF)
+    lo_write = pltpu.make_async_copy(lo_send, lo_hbm, out_sem.at[0])
+    lo_write.start()
+    for p in range(4):
+        seventh(p)
+
+    for p in range(4):
+        arrived(batch(first_recv, p, PIECES[p][0]), sum_ss.at[p, 4])
         arrived(gw.at[area(p, "", base=k * 256)], sum_ss.at[p, 5])
         gw_write(p, k).wait()
         gw_write(p, 1 - k).wait()
@@ -554,7 +562,8 @@
             [buf(16, 2048) if axes == "xz" else buf(64, 256) for axes in PIECES],
             [buf(8, 16, 256) if axes == "xz" else buf(4, 16, 256) for axes in PIECES],
             buf(4, 16, 256), buf(4, 16, 256),
-            dma((6,)), dma((11,)), dma, dma, dma((8,)), dma((8,)), dma((16,)), dma((16,)),
+            dma((6,)), dma((11,)), dma, dma, dma((8,)), dma((8,)), dma((8,)), dma((8,)),
+            dma((8,)), dma((8,)),
             dma((8,)), dma((8,)),
             dma((8,)), dma((8,)), dma((8,)), dma((8,)), dma, dma, dma((8,)), dma((8,)),
             dma((4,)), dma((4,)), dma, dma,

time: 93.3 us -> 92.5 us (level)
  no operation moved by 1% of the time
where the time goes in v6:
time: 92.5 us; the launch traced here: 92.4 us
  Pallas kernels  91.6 us (99%)
    pallas_call x1, Pallas kernels, on_device(): pl.pallas_call(main_kernel, out_shape=mid, in_specs=[any_spec] * 6, out_s...  87 us
    pallas_call x1, Pallas kernels, on_device(): pl.pallas_call(place_kernel, out_shape=(mid[0], grid, grid, grid, jax.Sha...  4.54 us

profile of v6, /device:TPU:1, one launch (start us, length us, event | category | flops | bytes accessed | tf_op | source)
XLA Modules:
  0.0 92.4 jit_solution(679595100571840487)
XLA Ops:
  0.6 87.0 %strip_attention.1 = (bf16[256,1024]{1,0:T(8,128)(2,1)}, bf16[8,128,128]{2,1,0:T(8,128)(2,1)}, bf16[8,2,128,128]{3,2,1,0:T(8,128)(2,1)}, bf16[512,2048]{1,0:T(8,128)(2,1)}) custom-call(s32[2,8]{1,0:T(2,128)} %bitcast.9, bf16[2,4,64,512]{3,2,1,0:T(8,128)(2,1)} %bitcast.14, bf16[2,4,64,512]{3,2,1,0:T(8,128)(2,1)} %bitcast.15, ...), custom_call_target="tpu_custom_call" | custom-call | flops 5000000000 | bytes 10485760 | tf_op jit(solution)/shard_map/strip_attention/pallas_call | solution.py:543
  87.7 4.5 %place_gradients.1 = (bf16[256,1024]{1,0:T(8,128)(2,1)}, f32[2,4,64,512]{3,2,1,0:T(8,128)}, f32[2,4,64,512]{3,2,1,0:T(8,128)}, f32[2,4,64,512]{3,2,1,0:T(8,128)}, f32[512,2048]{1,0:T(8,128)}) custom-call(s32[2,8]{1,0:T(2,128)} %bitcast.10, bf16[256,1024]{1,0:T(8,128)(2,1)} %get-tuple-element.14.lo_hbm, bf16[8,128,128]{2,1,0:T(8,128)(2,1)} %get-tuple-element.15.dq_hbm, ...), custom_call_target="tpu_custom_call" | custom-call | flops 100000000 | bytes 10485760 | tf_op jit(solution)/shard_map/place_gradients/pallas_call | solution.py:581

commit v7 on v6

--- a/solution.py
+++ b/solution.py
@@ -133,6 +133,9 @@
                       cam=(c + 9 - 2 * (unit & 1)) & 7, frame=frame_of(unit))
 
     each(8, lambda i: kv_copy(i).start())
+    loads[3].wait()
+    g_copy = remote(gfull.at[hh], gfull.at[hh], g_ss, g_rs, head=1 - hh)
+    g_copy.start()
 
     loads[2].wait()
     for side in range(2):
@@ -149,9 +152,6 @@
 
     own_copy(q_send, q_recv, q_rs).start()
     each(7, lambda i: half_copy(q_send, q_recv, q_ss, q_rs, i + 1).start())
-    loads[3].wait()
-    g_copy = remote(gfull.at[hh], gfull.at[hh], g_ss, g_rs, head=1 - hh)
-    g_copy.start()
 
     def arrived(ref, sem):
         pltpu.make_async_copy(ref, ref, sem).wait()
@@ -216,18 +216,6 @@
 
     each(4, forward)
 
-    arrived(gfull.at[1 - hh], g_rs)
-    loads[4].wait()
-    grad_attn = dot_nt(gfull[0], w[:, :1024]) + dot_nt(gfull[1], w[:, 1024:])
-    grad_attn = grad_attn.astype(BF)
-    for fr in range(2):
-        for s in range(2):
-            for h in range(4):
-                do_send[h * 2 + s, fr * 64:(fr + 1) * 64] = grad_attn[
-                    fr * 128 + s * 64:fr * 128 + s * 64 + 64, h * 128:(h + 1) * 128]
-    own_copy(do_send, do_recv, do_rs).start()
-    each(7, lambda i: half_copy(do_send, do_recv, do_ss, do_rs, i + 1).start())
-
     each(16, lambda i: turn(kt, i >> 3, i & 7, 0))
 
     each(8, lambda i: arrived(att_recv.at[i], att_rs.at[i]))
@@ -246,15 +234,28 @@
         return remote(core_send.at[part], core_recv.at[part], core_ss.at[p], core_rs.at[p],
                       frame=other_core)
 
-    def multiply():
+    columns = [pl.ds(pl.multiple_of(i * 1024, 1024), 1024) for i in (hh, 1 - hh)]
+
+    def multiply(i):
         theirs = a_t[pl.ds(pl.multiple_of((1 - k) * 256, 256), 256), :]
-        for j in range(2):
-            core_send[:, j * 1024:(j + 1) * 1024] = dot(theirs, gfull[j]).astype(BF)
-        for p in range(4):
-            core_copy(p).start()
         mine = a_t[pl.ds(pl.multiple_of(k * 256, 256), 256), :]
-        for j in range(2):
-            own[:, j * 1024:(j + 1) * 1024] = dot(mine, gfull[j])
+        features = gfull[hh if i == 0 else 1 - hh]
+        core_send[:, columns[i]] = dot(theirs, features).astype(BF)
+        if i == 1:
+            for p in range(4):
+                core_copy(p).start()
+        own[:, columns[i]] = dot(mine, features)
+
+    def cotangent():
+        grad_attn = lo_done[:, :512] + dot_nt(gfull[1 - hh], w[:, columns[1]])
+        grad_attn = grad_attn.astype(BF)
+        for fr in range(2):
+            for s in range(2):
+                for h in range(4):
+                    do_send[h * 2 + s, fr * 64:(fr + 1) * 64] = grad_attn[
+                        fr * 128 + s * 64:fr * 128 + s * 64 + 64, h * 128:(h + 1) * 128]
+        own_copy(do_send, do_recv, do_rs).start()
+        each(7, lambda i: half_copy(do_send, do_recv, do_ss, do_rs, i + 1).start())
 
     def peers(axis):
         if axis == "x":
@@ -386,7 +387,12 @@
 
     far, near = 1 - k, k
 
-    multiply()
+    loads[4].wait()
+    lo_done[:, :512] = dot_nt(gfull[hh], w[:, columns[0]])
+    multiply(0)
+    arrived(gfull.at[1 - hh], g_rs)
+    multiply(1)
+    cotangent()
     first(0)
     first(1)
     for i in range(4):

time: 92.5 us -> 105 us (1.14)
  Pallas kernels: 91.6 us -> 104 us
    pallas_call x1, Pallas kernels: 87 us -> 99.4 us  [on_device(): pl.pallas_call(main_kernel, out_shape=mid, in_specs=[any_spec] * 6, out_s...]
where the time goes in v7:
time: 105 us
  Pallas kernels  104 us (99%)
    pallas_call x1, Pallas kernels, on_device(): pl.pallas_call(main_kernel, out_shape=mid, in_specs=[any_spec] * 6, out_s...  99.4 us
    pallas_call x1, Pallas kernels, on_device(): pl.pallas_call(place_kernel, out_shape=(mid[0], grid, grid, grid, jax.Sha...  4.54 us

profile of v7, /device:TPU:1, one launch (start us, length us, event | category | flops | bytes accessed | tf_op | source)
XLA Modules:
  0.0 104.7 jit_solution(15321423508328168677)
XLA Ops:
  0.6 99.4 %strip_attention.1 = (bf16[256,1024]{1,0:T(8,128)(2,1)}, bf16[8,128,128]{2,1,0:T(8,128)(2,1)}, bf16[8,2,128,128]{3,2,1,0:T(8,128)(2,1)}, bf16[512,2048]{1,0:T(8,128)(2,1)}) custom-call(s32[2,8]{1,0:T(2,128)} %bitcast.9, bf16[2,4,64,512]{3,2,1,0:T(8,128)(2,1)} %bitcast.14, bf16[2,4,64,512]{3,2,1,0:T(8,128)(2,1)} %bitcast.15, ...), custom_call_target="tpu_custom_call" | custom-call | flops 5000000000 | bytes 10485760 | tf_op jit(solution)/shard_map/strip_attention/pallas_call | solution.py:549
  100.0 4.5 %place_gradients.1 = (bf16[256,1024]{1,0:T(8,128)(2,1)}, f32[2,4,64,512]{3,2,1,0:T(8,128)}, f32[2,4,64,512]{3,2,1,0:T(8,128)}, f32[2,4,64,512]{3,2,1,0:T(8,128)}, f32[512,2048]{1,0:T(8,128)}) custom-call(s32[2,8]{1,0:T(2,128)} %bitcast.10, bf16[256,1024]{1,0:T(8,128)(2,1)} %get-tuple-element.14.lo_hbm, bf16[8,128,128]{2,1,0:T(8,128)(2,1)} %get-tuple-element.15.dq_hbm, ...), custom_call_target="tpu_custom_call" | custom-call | flops 100000000 | bytes 10485760 | tf_op jit(solution)/shard_map/place_gradients/pallas_call | solution.py:587

commit v8 on v7

--- a/solution.py
+++ b/solution.py
@@ -13,7 +13,9 @@
 MESH = pl.DeviceIdType.MESH
 LOG2E = 1.4426950408889634
 NT = (((1,), (1,)), ((), ()))
-PIECES = ("xz", "zx", "xz", "xz")
+PIECES = ("xz", "zx", "xz")
+ROWS = (64, 64, 128)
+START = (0, 64, 128)
 
 
 def dot(a, b):
@@ -133,9 +135,6 @@
                       cam=(c + 9 - 2 * (unit & 1)) & 7, frame=frame_of(unit))
 
     each(8, lambda i: kv_copy(i).start())
-    loads[3].wait()
-    g_copy = remote(gfull.at[hh], gfull.at[hh], g_ss, g_rs, head=1 - hh)
-    g_copy.start()
 
     loads[2].wait()
     for side in range(2):
@@ -152,6 +151,9 @@
 
     own_copy(q_send, q_recv, q_rs).start()
     each(7, lambda i: half_copy(q_send, q_recv, q_ss, q_rs, i + 1).start())
+    loads[3].wait()
+    g_copy = remote(gfull.at[hh], gfull.at[hh], g_ss, g_rs, head=1 - hh)
+    g_copy.start()
 
     def arrived(ref, sem):
         pltpu.make_async_copy(ref, ref, sem).wait()
@@ -230,7 +232,7 @@
                 a_rows[fr * 128:(fr + 1) * 128, h * 128:(h + 1) * 128]).astype(BF)
 
     def core_copy(p):
-        part = pl.ds(p * 64, 64)
+        part = pl.ds(START[p], ROWS[p])
         return remote(core_send.at[part], core_recv.at[part], core_ss.at[p], core_rs.at[p],
                       frame=other_core)
 
@@ -242,7 +244,7 @@
         features = gfull[hh if i == 0 else 1 - hh]
         core_send[:, columns[i]] = dot(theirs, features).astype(BF)
         if i == 1:
-            for p in range(4):
+            for p in range(3):
                 core_copy(p).start()
         own[:, columns[i]] = dot(mine, features)
 
@@ -263,11 +265,12 @@
         return [((c + i) & 7, dict(cam=(c + i) & 7)) for i in (1, 7, 2, 6, 3, 5, 4)]
 
     def area(p, axes, at_x=x, at_z=c, base=0):
-        rows, cols = pl.ds(base + p * 64, 64), pl.ds(0, 2048)
+        first_row, count = base + START[p], ROWS[p]
+        rows, cols = pl.ds(first_row, count), pl.ds(0, 2048)
         if "x" in axes:
-            rows = pl.ds(pl.multiple_of(base + p * 64 + at_x * 16, 16), 16)
+            rows = pl.ds(pl.multiple_of(first_row + at_x * (count // 4), 16), count // 4)
         elif not isinstance(base, int):
-            rows = pl.ds(pl.multiple_of(base + p * 64, 64), 64)
+            rows = pl.ds(pl.multiple_of(first_row, 64), count)
         if "z" in axes:
             cols = pl.ds(pl.multiple_of(at_z * 256, 256), 256)
         return rows, cols
@@ -285,7 +288,7 @@
         arrived(batch(first_recv, p, PIECES[p][0]), sum_ss.at[p, 0])
 
     def first(p):
-        part = pl.ds(p * 64, 64)
+        part = pl.ds(START[p], ROWS[p])
         axis = PIECES[p][0]
         arrived(core_recv.at[part], core_rs.at[p])
         own[part, :] += core_recv[part, :].astype(F32)
@@ -307,10 +310,10 @@
     def mid_part(p, to):
         if PIECES[p][1] == "x":
             return pl.ds(pl.multiple_of(to * 16, 16), 16), pl.ds(0, 256)
-        return pl.ds(0, 16), pl.ds(pl.multiple_of(to * 256, 256), 256)
+        return pl.ds(0, ROWS[p] // 4), pl.ds(pl.multiple_of(to * 256, 256), 256)
 
     def y_copy(p):
-        return sum_copy(y_send.at[p], y_recv.at[p], p, 2, dict(frame=other_half))
+        return sum_copy(y_send[p], y_recv[p], p, 2, dict(frame=other_half))
 
     def third(p):
         axis = PIECES[p][1]
@@ -318,7 +321,7 @@
         total = mid_sum[p][mid_part(p, me(axis))].astype(F32)
         for frm, _ in peers(axis):
             total = total + second_recv[p][frm].astype(F32)
-        y_send[p] = total.astype(BF)
+        y_send[p][...] = total.astype(BF)
         y_copy(p).start()
 
     def gather(p, axes, axis, step):
@@ -327,9 +330,9 @@
             sum_copy(part, part, p, step, where).start()
 
     def fourth(p):
-        arrived(y_recv.at[p], sum_rs.at[p, 2])
+        arrived(y_recv[p], sum_rs.at[p, 2])
         gw[area(p, "xz", base=k * 256)] = (
-            y_send[p].astype(F32) + y_recv[p].astype(F32)).astype(BF)
+            y_send[p][...].astype(F32) + y_recv[p][...].astype(F32)).astype(BF)
         gather(p, "xz", PIECES[p][1], 3)
 
     def fifth(p):
@@ -395,20 +398,26 @@
     cotangent()
     first(0)
     first(1)
-    for i in range(4):
-        backward(far, i)
+    first(2)
+    lo_send[...] = dot(
+        a_rows[...], w[:, pl.ds(pl.multiple_of((1 - hh) * 1024, 1024), 1024)]).astype(BF)
+    lo_copy = remote(lo_send, lo_recv, lo_ss, lo_rs, head=1 - hh)
+    lo_copy.start()
+    backward(far, 0)
+    backward(far, 1)
+    backward(far, 2)
+    backward(far, 3)
     far_send[:, 0] = dk_acc[...].astype(BF).reshape(8, 128, 128)
     far_send[:, 1] = dv_acc[...].astype(BF).reshape(8, 128, 128)
     far_copy().start()
-    first_sent(0)
-    first(2)
+    second(0)
+    second(1)
     backward(near, 0)
-    second(0)
+    second(2)
     backward(near, 1)
-    first_sent(2)
-    first(3)
+    third(0)
+    third(1)
     backward(near, 2)
-    second(1)
     backward(near, 3)
     far_copy().wait()
     for i, acc in enumerate((dk_acc, dv_acc)):
@@ -417,24 +426,13 @@
             total = total * scale
         dkv_send[:, i] = total.astype(BF)
     each(8, lambda i: dkv_copy(i).start())
-    second(2)
-    third(0)
-    second(3)
-    third(1)
+    fourth(0)
+    fourth(1)
     third(2)
-    fourth(0)
-    third(3)
-    fourth(1)
     fourth(2)
-    fourth(3)
-    lo_send[...] = dot(
-        a_rows[...], w[:, pl.ds(pl.multiple_of((1 - hh) * 1024, 1024), 1024)]).astype(BF)
-    lo_copy = remote(lo_send, lo_recv, lo_ss, lo_rs, head=1 - hh)
-    lo_copy.start()
     fifth(0)
     fifth(1)
     fifth(2)
-    fifth(3)
 
     lo_done[...] = dot(
         a_rows[...], w[:, pl.ds(pl.multiple_of(hh * 1024, 1024), 1024)])
@@ -456,9 +454,9 @@
     sent(att_send, att_recv, att_ss, att_rs)
     sent(dq_send, dq_recv, dq_ss, dq_rs)
     each(8, lambda i: dkv_copy(i).wait_send())
-    first_sent(1)
-    first_sent(3)
-    for p in range(4):
+    for p in range(3):
+        first_sent(p)
+    for p in range(3):
         core_copy(p).wait_send()
         arrived(batch(second_recv, p, PIECES[p][1]), sum_ss.at[p, 1])
         y_copy(p).wait_send()
@@ -466,15 +464,14 @@
     sixth(0)
     sixth(1)
     sixth(2)
-    sixth(3)
     lo_copy.wait()
     lo_send[...] = (lo_done[...] + lo_recv[...].astype(F32)).astype(BF)
     lo_write = pltpu.make_async_copy(lo_send, lo_hbm, out_sem.at[0])
     lo_write.start()
-    for p in range(4):
+    for p in range(3):
         seventh(p)
 
-    for p in range(4):
+    for p in range(3):
         arrived(batch(first_recv, p, PIECES[p][0]), sum_ss.at[p, 4])
         arrived(gw.at[area(p, "", base=k * 256)], sum_ss.at[p, 5])
         gw_write(p, k).wait()
@@ -564,10 +561,10 @@
             buf(256, 512), buf(512, 256), buf(256, 2048), buf(256, 2048),
             pltpu.VMEM((256, 2048), F32), buf(256, 1024), buf(256, 1024), pltpu.VMEM((256, 1024), F32),
             buf(256, 2048), buf(512, 2048),
-            [buf(4, 16, 2048) if axes == "xz" else buf(8, 64, 256) for axes in PIECES],
-            [buf(16, 2048) if axes == "xz" else buf(64, 256) for axes in PIECES],
-            [buf(8, 16, 256) if axes == "xz" else buf(4, 16, 256) for axes in PIECES],
-            buf(4, 16, 256), buf(4, 16, 256),
+            [buf(4, n // 4, 2048) if axes == "xz" else buf(8, n, 256) for axes, n in zip(PIECES, ROWS)],
+            [buf(n // 4, 2048) if axes == "xz" else buf(n, 256) for axes, n in zip(PIECES, ROWS)],
+            [buf(8 if axes == "xz" else 4, n // 4, 256) for axes, n in zip(PIECES, ROWS)],
+            [buf(n // 4, 256) for n in ROWS], [buf(n // 4, 256) for n in ROWS],
             dma((6,)), dma((11,)), dma, dma, dma((8,)), dma((8,)), dma((8,)), dma((8,)),
             dma((8,)), dma((8,)),
             dma((8,)), dma((8,)),

time: 105 us -> 89 us (0.85)
  Pallas kernels: 104 us -> 88.1 us
    pallas_call x1, Pallas kernels: 99.4 us -> 83.6 us  [on_device(): pl.pallas_call(main_kernel, out_shape=mid, in_specs=[any_spec] * 6, out_s...]
where the time goes in v8:
time: 89 us; the launch traced here: 88.9 us
  Pallas kernels  88.1 us (99%)
    pallas_call x1, Pallas kernels, on_device(): pl.pallas_call(main_kernel, out_shape=mid, in_specs=[any_spec] * 6, out_s...  83.6 us
    pallas_call x1, Pallas kernels, on_device(): pl.pallas_call(place_kernel, out_shape=(mid[0], grid, grid, grid, jax.Sha...  4.54 us

profile of v8, /device:TPU:1, one launch (start us, length us, event | category | flops | bytes accessed | tf_op | source)
XLA Modules:
  0.0 88.9 jit_solution(11859531241574465032)
XLA Ops:
  0.6 83.6 %strip_attention.1 = (bf16[256,1024]{1,0:T(8,128)(2,1)}, bf16[8,128,128]{2,1,0:T(8,128)(2,1)}, bf16[8,2,128,128]{3,2,1,0:T(8,128)(2,1)}, bf16[512,2048]{1,0:T(8,128)(2,1)}) custom-call(s32[2,8]{1,0:T(2,128)} %bitcast.9, bf16[2,4,64,512]{3,2,1,0:T(8,128)(2,1)} %bitcast.14, bf16[2,4,64,512]{3,2,1,0:T(8,128)(2,1)} %bitcast.15, ...), custom_call_target="tpu_custom_call" | custom-call | flops 5000000000 | bytes 10485760 | tf_op jit(solution)/shard_map/strip_attention/pallas_call | solution.py:546
  84.2 4.5 %place_gradients.1 = (bf16[256,1024]{1,0:T(8,128)(2,1)}, f32[2,4,64,512]{3,2,1,0:T(8,128)}, f32[2,4,64,512]{3,2,1,0:T(8,128)}, f32[2,4,64,512]{3,2,1,0:T(8,128)}, f32[512,2048]{1,0:T(8,128)}) custom-call(s32[2,8]{1,0:T(2,128)} %bitcast.10, bf16[256,1024]{1,0:T(8,128)(2,1)} %get-tuple-element.14.lo_hbm, bf16[8,128,128]{2,1,0:T(8,128)(2,1)} %get-tuple-element.15.dq_hbm, ...), custom_call_target="tpu_custom_call" | custom-call | flops 100000000 | bytes 10485760 | tf_op jit(solution)/shard_map/place_gradients/pallas_call | solution.py:584

commit v9 on v8

--- a/solution.py
+++ b/solution.py
@@ -57,7 +57,7 @@
     lo_hbm, dq_hbm, dkv_hbm, gw_hbm,
     offs, q_in, k_in, v_in, w, gfull,
     q_send, kv_send, do_send, q_recv, kv_recv, do_recv,
-    kt, vt, probs, o_t, rl,
+    kt, vt, probs, o_t, rl, grads_t,
     att_send, att_recv, dq_acc, dq_send, dq_recv, dk_acc, dv_acc, far_send, far_recv, dkv_send, dkv_recv,
     a_rows, a_t, core_send, core_recv, own, lo_send, lo_recv, lo_done,
     out_bf, gw, first_recv, mid_sum, second_recv, y_send, y_recv,
@@ -360,10 +360,14 @@
                 arrived(do_recv.at[2 * b + t], do_rs.at[2 * b + t])
         queries = q_recv[pl.ds(2 * b, 2)].reshape(256, 128)
         weights = probs[half, b]
-        grad_t = transposed(do_recv[pl.ds(2 * b, 2)].reshape(256, 128)) * rl[b]
-        delta = jnp.sum(grad_t * o_t[b], axis=0, keepdims=True)
-        grads = grad_t.T.astype(BF)
-        grad_probs = dot(stacked(half, 1), grad_t.astype(BF))
+        if half is far:
+            grad_t = transposed(do_recv[pl.ds(2 * b, 2)].reshape(256, 128)) * rl[b]
+            rl[b] = jnp.sum(grad_t * o_t[b], axis=0, keepdims=True)
+            grads_t[b] = grad_t.astype(BF)
+            do_recv[pl.ds(2 * b, 2)] = grad_t.T.astype(BF).reshape(2, 128, 128)
+        delta = rl[b]
+        grads = do_recv[pl.ds(2 * b, 2)].reshape(256, 128)
+        grad_probs = dot(stacked(half, 1), grads_t[b])
         grad_scores = (weights.astype(F32) * (grad_probs - delta)).astype(BF)
         grad_q_t = dot(kt[half], grad_scores)
         if half is far:
@@ -554,7 +558,7 @@
             buf(8, *tile), buf(8, 2, *tile), buf(8, *tile),
             buf(8, *tile), buf(2, 8, 2, *tile), buf(8, *tile),
             buf(2, 128, 1024), buf(2, 128, 1024), buf(2, 4, 1024, 256),
-            pltpu.VMEM((4, 128, 256), F32), pltpu.VMEM((4, 1, 256), F32),
+            pltpu.VMEM((4, 128, 256), F32), pltpu.VMEM((4, 1, 256), F32), buf(4, 128, 256),
             buf(8, *tile), buf(8, *tile), pltpu.VMEM((4, 128, 256), F32), buf(8, *tile), buf(8, *tile),
             pltpu.VMEM((1024, 128), F32), pltpu.VMEM((1024, 128), F32),
             buf(8, 2, *tile), buf(8, 2, *tile), buf(8, 2, *tile), buf(8, 2, *tile),

time: 89 us -> 89.2 us (level)
  no operation moved by 1% of the time
where the time goes in v9:
time: 89.2 us; the launch traced here: 88.9 us
  Pallas kernels  88.1 us (99%)
    pallas_call x1, Pallas kernels, on_device(): pl.pallas_call(main_kernel, out_shape=mid, in_specs=[any_spec] * 6, out_s...  83.6 us
    pallas_call x1, Pallas kernels, on_device(): pl.pallas_call(place_kernel, out_shape=(mid[0], grid, grid, grid, jax.Sha...  4.54 us

profile of v9, /device:TPU:1, one launch (start us, length us, event | category | flops | bytes accessed | tf_op | source)
XLA Modules:
  0.0 88.9 jit_solution(4897869704568123626)
XLA Ops:
  0.6 83.6 %strip_attention.1 = (bf16[256,1024]{1,0:T(8,128)(2,1)}, bf16[8,128,128]{2,1,0:T(8,128)(2,1)}, bf16[8,2,128,128]{3,2,1,0:T(8,128)(2,1)}, bf16[512,2048]{1,0:T(8,128)(2,1)}) custom-call(s32[2,8]{1,0:T(2,128)} %bitcast.9, bf16[2,4,64,512]{3,2,1,0:T(8,128)(2,1)} %bitcast.14, bf16[2,4,64,512]{3,2,1,0:T(8,128)(2,1)} %bitcast.15, ...), custom_call_target="tpu_custom_call" | custom-call | flops 5000000000 | bytes 10485760 | tf_op jit(solution)/shard_map/strip_attention/pallas_call | solution.py:550
  84.2 4.5 %place_gradients.1 = (bf16[256,1024]{1,0:T(8,128)(2,1)}, f32[2,4,64,512]{3,2,1,0:T(8,128)}, f32[2,4,64,512]{3,2,1,0:T(8,128)}, f32[2,4,64,512]{3,2,1,0:T(8,128)}, f32[512,2048]{1,0:T(8,128)}) custom-call(s32[2,8]{1,0:T(2,128)} %bitcast.10, bf16[256,1024]{1,0:T(8,128)(2,1)} %get-tuple-element.14.lo_hbm, bf16[8,128,128]{2,1,0:T(8,128)(2,1)} %get-tuple-element.15.dq_hbm, ...), custom_call_target="tpu_custom_call" | custom-call | flops 100000000 | bytes 10485760 | tf_op jit(solution)/shard_map/place_gradients/pallas_call | solution.py:588
